TPU v7x, 512 devices: a whole 4x8x8 slice. The times are simulated.
512 devices in a mesh: rows: 64 (over z, y_lo, x), feat: 8 (over y_hi, core).
Axes of the slice: x: 4, y: 8 (y_hi: 4, y_lo: 2; y = y_hi * 2 + y_lo), z: 8, core: 2. Of those that a mesh axis runs over, the one named last changes fastest.
Arguments:
- train_grads: bfloat16 [32768, 2, 128, 128], P('rows', None, 'feat'), may hold values from -0.03125 to 0.03125
- query_grads: bfloat16 [512, 2, 128, 128], P('rows', None, 'feat'), may hold values from -6 to 6
- out_inv: float32 [2, 128, 128], replicated, may hold values from -1 to 2, as said below
- in_inv: float32 [2, 128, 128], replicated, may hold values from -1 to 2, as said below
Outputs:
- scores: float32 [32768, 512], P('rows', 'feat')
Inputs may be any that keep to these rules, and one draw needn't show every extreme that they name: `out_inv`: symmetric, with diagonal between 1 and 2 and small off-diagonal entries; positive definite. `in_inv`: symmetric, with diagonal between 1 and 2 and small off-diagonal entries; positive definite.
All inputs are finite; a program needn't handle non-finite values.
Results may differ from a plain program's by a relative error of at most 0.0029.
Values may be sent and summed in bfloat16 or wider, within the bound.
No kernel may reach another device: no remote copies, remote signals or barrier semaphores. Data moves between devices by JAX's collectives and lax.ppermute only.
A program may use at most 64 MiB of HBM per device.

v0:
```python
import jax
import jax.numpy as jnp
from jax import lax
from jax.sharding import PartitionSpec as P


def body(train_grads, query_grads, out_inv, in_inv):
    highest = lax.Precision.HIGHEST
    out_dev = query_grads.shape[2]
    feat_index = lax.axis_index("feat")
    mid = jnp.einsum("qloi,lik->qlok", query_grads.astype(jnp.float32), in_inv, precision=highest)
    own_rows = lax.dynamic_slice_in_dim(out_inv, feat_index * out_dev, out_dev, 1)
    mixed = jnp.einsum(
        "loj,qljk->qlok",
        own_rows,
        lax.all_gather(mid, "feat", axis=2, tiled=True),
        precision=highest,
    )
    precond = mixed.astype(jnp.bfloat16)
    train_flat = train_grads.reshape(train_grads.shape[0], -1)
    piece = lax.all_gather(precond, "rows", axis=0, tiled=True)
    flat_piece = piece.reshape(piece.shape[0], -1)
    partial_scores = lax.dot_general(
        train_flat, flat_piece, (((1,), (1,)), ((), ())), preferred_element_type=jnp.float32
    )
    return lax.psum_scatter(partial_scores, "feat", scatter_dimension=1, tiled=True)


def solution(mesh):
    placed = (P("rows", None, "feat", None), P("rows", None, "feat", None), P(), P())
    return jax.shard_map(
        body, mesh=mesh, in_specs=placed, out_specs=P("rows", "feat"), check_vma=False
    )
```

profile of v0, /device:TPU:1, one launch (start us, length us, event | category | flops | bytes accessed | tf_op | source)
XLA Modules:
  0.0 348.8 jit_solution(12142066648558860045)
XLA Ops:
  6.5 0.0 copy-start
  6.5 0.0 all-gather.3.cloned.1.call-start
  6.5 0.9 copy-done
  7.4 1.7 convolution_bitcast_fusion
  9.2 0.0 all-gather.3.cloned.1.call-update
  9.2 0.0 all-gather.5.cloned.1.call-start
  9.2 38.4 %all-gather.3.cloned.1.call-done = f32[8,2,128,128]{3,0,1,2:T(8,128)} async-done(((f32[8,2,16,128]{3,0,1,2:T(8,128)}), f32[8,2,128,128]{3,0,1,2:T(8,128)}) %all-gather.3.cloned.1.call-update) | async-done | bytes 1048592 | tf_op jit(solution)/shard_map/all_gather | solution.py:16
  47.7 2.1 fusion.5
  49.8 0.6 copy.23
  50.5 0.0 all-gather.5.cloned.1.call-update
  50.5 0.0 reduce-scatter.2.cloned.1.call-start
  50.5 213.2 %all-gather.5.cloned.1.call-done = bf16[512,2,16,128]{3,0,2,1:T(8,128)(2,1)} async-done(((bf16[8,2,16,128]{3,0,2,1:T(8,128)(2,1)}), bf16[512,2,16,128]{3,0,2,1:T(8,128)(2,1)}) %all-gather.5.cloned.1.call-update) | async-done | bytes 4194320 | tf_op jit(solution)/shard_map/all_gather | solution.py:21
  263.7 7.3 %fusion.2 = f32[512,512]{0,1:T(8,128)} fusion(bf16[512,2,16,128]{3,0,2,1:T(8,128)(2,1)} %all-gather.5.cloned.1.call-done, bf16[512,2,16,128]{3,2,1,0:T(8,128)(2,1)} %param.4), kind=kOutput, calls=%fused_computation.2 | convolution fusion | flops 2147483648 | bytes 9437184 | tf_op jit(solution)/shard_map/dot_general | solution.py:23
  271.0 0.0 reduce-scatter.2.cloned.1.call-update
  271.0 71.2 %reduce-scatter.2.cloned.1.call-done = f32[512,64]{0,1:T(8,128)} async-done(((f32[512,512]{0,1:T(8,128)}), f32[512,64]{0,1:T(8,128)}) %reduce-scatter.2.cloned.1.call-update) | async-done | bytes 131088 | tf_op jit(solution)/shard_map/reduce_scatter | solution.py:26
Async XLA Ops:
  6.5 0.9 copy-start
  6.5 41.1 %all-gather.3.cloned.1.call-start = ((), (), s32[]{:S(2)}) async-start(), calls=%async_computation.1 | async-start | bytes 1179648 | tf_op jit(solution)/shard_map/all_gather | solution.py:16
  9.2 254.5 %all-gather.5.cloned.1.call-start = ((), (), s32[]{:S(2)}) async-start(), calls=%async_computation.2 | async-start | bytes 4259840 | tf_op jit(solution)/shard_map/all_gather | solution.py:21
  50.5 291.7 %reduce-scatter.2.cloned.1.call-start = ((), (), s32[]{:S(2)}) async-start(), calls=%async_computation.3 | async-start | bytes 1179648 | tf_op jit(solution)/shard_map/reduce_scatter | solution.py:26
Sparse Core Ops, SparseCore 0:
  9.5 38.1 all-gather.2
  50.6 213.0 all-gather.4
  271.2 71.0 reduce-scatter.1
where the time goes:
time: 350 us; the launch traced here: 349 us
  waiting for transfers between devices  323 us (92%)
  between operations  13.1 us (4%)
  matrix products  11.1 us (3%)
    all_gather x1, waiting for transfers between devices, body(): piece = lax.all_gather(precond, 'rows', axis=0, tiled=True)  213 us
    reduce_scatter x1, waiting for transfers between devices, body(): lax.psum_scatter(partial_scores, 'feat', scatter_dimension=1, tiled=True)  71.2 us
    all_gather x1, waiting for transfers between devices, body(): lax.all_gather(mid, 'feat', axis=2, tiled=True)  38.4 us
    dot_general x1, matrix products, body(): lax.dot_general(train_flat, flat_piece, (((1,), (1,)), ((), ())), preferr...  7.3 us
  transfers between devices with their start and end apart: 3, of which 3 were waited for; matrix products, arithmetic and copies ran while one was open for 0% of the time, Pallas kernels for 0%

commit v1 on v0

v1 whole, which is shorter than its diff:
```python
import functools

import jax
import jax.numpy as jnp
from jax import lax
from jax.experimental import pallas as pl
from jax.experimental.pallas import tpu as pltpu
from jax.sharding import Mesh
from jax.sharding import PartitionSpec as P

NAMES = ("zh", "zl", "yl", "x", "yh", "c")
SIZES = (2, 4, 2, 4, 4, 2)
FEAT = ("yh", "c")
NEAR = {0: (1, 3), 1: (3, 1)}
MASKS = {0: (0, 1, 3, 2), 1: (0, 3, 1, 2)}


def device_index(zh, zl, yl, x, yh, c):
    index = 0
    for size, at in zip(SIZES, (zh, zl, yl, x, yh, c)):
        index = index * size + at
    return index


def step_pairs(axis, step):
    pairs = []
    for z in range(8):
        for yl in range(2):
            for x in range(4):
                for yh in range(4):
                    for c in range(2):
                        mask = NEAR[c][step]
                        z2, x2 = z, x
                        if axis == "x":
                            x2 = x ^ mask
                        elif mask == 1:
                            z2 = z ^ 1
                        else:
                            z2 = (z + (1 if z % 2 else -1)) % 8
                        pairs.append(
                            (
                                device_index(z // 4, z % 4, yl, x, yh, c),
                                device_index(z2 // 4, z2 % 4, yl, x2, yh, c),
                            )
                        )
    return pairs


def exchange(block, axis, step):
    return lax.ppermute(block, NAMES, step_pairs(axis, step))


def precond_kernel(q_ref, out_inv_ref, in_inv_ref, send_ref):
    for layer in range(2):
        whole = q_ref[:, layer].astype(jnp.float32).reshape(128, 128)
        mid = jnp.dot(
            whole, in_inv_ref[layer], precision=lax.Precision.HIGHEST, preferred_element_type=jnp.float32
        )
        mixed = jnp.dot(
            out_inv_ref[layer], mid, precision=lax.Precision.HIGHEST, preferred_element_type=jnp.float32
        )
        mixed = mixed.astype(jnp.bfloat16).reshape(8, 16, 128)
        for copy in range(send_ref.shape[0]):
            send_ref[copy, :, layer] = mixed


def precondition(raw, out_inv, in_inv):
    return pl.pallas_call(
        precond_kernel,
        out_shape=jax.ShapeDtypeStruct((4, 8, 2, 16, 128), jnp.bfloat16),
        cost_estimate=pl.CostEstimate(flops=200_000_000, bytes_accessed=700_000, transcendentals=0),
    )(raw, out_inv, in_inv)


def nt_dot(a, b):
    return lax.dot_general(a, b, (((1,), (1,)), ((), ())), preferred_element_type=jnp.float32)


def early_kernel(pre_a_ref, pre_b_ref, train_ref, out_ref):
    out_ref[:128] = nt_dot(pre_a_ref[...], train_ref[...]).astype(jnp.bfloat16)
    out_ref[128:] = nt_dot(pre_b_ref[...], train_ref[...]).astype(jnp.bfloat16)


def late_kernel(place_ref, early_ref, pre_a_ref, pre_b_ref, train_ref, send_ref):
    for half, pre_ref in ((0, pre_a_ref), (1, pre_b_ref)):
        scores = nt_dot(pre_ref[...], train_ref[...]).astype(jnp.bfloat16)
        for block in range(8):
            send_ref[place_ref[half * 16 + block]] = early_ref[pl.ds(half * 128 + block * 16, 16)]
            send_ref[place_ref[half * 16 + 8 + block]] = scores[block * 16 : block * 16 + 16]


def early_scores(pre_a, pre_b, train):
    return pl.pallas_call(
        early_kernel,
        out_shape=jax.ShapeDtypeStruct((256, 512), jnp.bfloat16),
        cost_estimate=pl.CostEstimate(flops=1_073_741_824, bytes_accessed=7_000_000, transcendentals=0),
        compiler_params=pltpu.CompilerParams(vmem_limit_bytes=32 * 1024 * 1024),
    )(pre_a, pre_b, train)


def late_scores(place, early, pre_a, pre_b, train):
    whole = pl.BlockSpec(memory_space=pltpu.VMEM)
    return pl.pallas_call(
        late_kernel,
        out_shape=jax.ShapeDtypeStruct((32, 16, 512), jnp.bfloat16),
        in_specs=[pl.BlockSpec(memory_space=pltpu.SMEM)] + [whole] * 4,
        out_specs=whole,
        cost_estimate=pl.CostEstimate(flops=1_073_741_824, bytes_accessed=7_000_000, transcendentals=0),
        compiler_params=pltpu.CompilerParams(vmem_limit_bytes=32 * 1024 * 1024),
    )(place, early, pre_a, pre_b, train)


def body(train_grads, query_grads, out_inv, in_inv):
    raw = lax.all_to_all(query_grads, FEAT, 0, 0, tiled=True)
    send = precondition(raw, out_inv, in_inv)
    held = lax.all_to_all(send.reshape(32, 32, 128), ("zh", "yl", "yh", "c"), 0, 0, tiled=True)
    held = held.reshape(32, 4096)
    train = train_grads.reshape(512, 4096)
    a, b = held[:16], held[16:]
    for axes in (("x", "zl"), ("zl", "x")):
        pass
    for step in range(2):
        got_a, got_b = exchange(a, "x", step), exchange(b, "zl", step)
        a, b = jnp.concatenate([a, got_a]), jnp.concatenate([b, got_b])
    got_a, got_b = exchange(a, "zl", 0), exchange(b, "x", 0)
    a, b = jnp.concatenate([a, got_a]), jnp.concatenate([b, got_b])
    got_a, got_b = exchange(a, "zl", 1), exchange(b, "x", 1)
    early = early_scores(a, b, train)

    core, x, zl = lax.axis_index("c"), lax.axis_index("x"), lax.axis_index("zl")
    masks = jnp.where(core == 0, jnp.array(MASKS[0], jnp.int32), jnp.array(MASKS[1], jnp.int32))
    x_of, z_of = x ^ masks, zl ^ masks
    place_a = (z_of[:, None] * 4 + x_of[None, :]).reshape(16)
    place_b = (16 + z_of[None, :] * 4 + x_of[:, None]).reshape(16)
    place = jnp.concatenate([place_a, place_b]).astype(jnp.int32)

    partial = late_scores(place, early, got_a, got_b, train)
    parts = lax.all_to_all(partial.reshape(8, 64, 512), FEAT, 0, 0, tiled=True)
    total = jnp.sum(parts.astype(jnp.float32), axis=0)
    total = total.reshape(4, 2, 8, 512).transpose(1, 0, 2, 3).reshape(64, 512)
    return total.T


def solution(mesh):
    fine = Mesh(mesh.devices.reshape(SIZES), NAMES)
    rows, feat = ("zh", "zl", "yl", "x"), FEAT
    placed = (P(rows, None, feat, None), P(rows, None, feat, None), P(), P())
    return jax.shard_map(
        body, mesh=fine, in_specs=placed, out_specs=P(rows, feat), check_vma=False
    )
```

time: 350 us -> 121 us (0.35)
  waiting for transfers between devices: 323 us -> 11.2 us
  blocking collectives: 0 us -> 66.2 us
  starting transfers between devices: 0.09 us -> 22.8 us
  between operations: 13.1 us -> 0.24 us
  matrix products: 11.1 us -> 0 us
  Pallas kernels: 0 us -> 9.28 us
  local copies, waits for them, and re-layouts: 1.55 us -> 9.61 us
    all_gather x2 -> x0, waiting for transfers between devices: 252 us -> none  [the longest x1 213 us: body(): piece = lax.all_gather(precond, 'rows', axis=0, tiled=True)]
    reduce_scatter x1 -> x0, waiting for transfers between devices: 71.2 us -> none  [body(): lax.psum_scatter(partial_scores, 'feat', scatter_dimension=1, tiled=True)]
    all_to_all x0 -> x3, blocking collectives: none -> 66.2 us  [the longest x1 25.7 us: body(): lax.all_to_all(send.reshape(32, 32, 128), ('zh', 'yl', 'yh', 'c'), 0, 0,...]
    ppermute x0 -> x8, starting transfers between devices: none -> 22.8 us  [exchange(): return lax.ppermute(block, NAMES, step_pairs(axis, step))]
    ppermute x0 -> x8, waiting for transfers between devices: none -> 11.2 us  [exchange(): return lax.ppermute(block, NAMES, step_pairs(axis, step))]
    dot_general x3 -> x0, matrix products: 11.1 us -> none  [the longest x1 7.3 us: body(): lax.dot_general(train_flat, flat_piece, (((1,), (1,)), ((), ())), preferr...]
    pallas_call x0 -> x3, Pallas kernels: none -> 9.28 us  [the longest x1 4.13 us: late_scores(): pl.pallas_call(late_kernel, out_shape=jax.ShapeDtypeStruct((32, 16, 512),...]
    unnamed x2 -> x19, local copies, waits for them, and re-layouts: 0.9 us -> 8.7 us
  transfers between devices with their start and end apart: 3 -> 8, of which waited for: 3 -> 5; matrix products, arithmetic and copies ran while one was open for 0% -> 6% of each run, Pallas kernels for 0% -> 2%
where the time goes in v1:
time: 121 us; the launch traced here: 120 us
  blocking collectives  66.2 us (55%)
  starting transfers between devices  22.8 us (19%)
  waiting for transfers between devices  11.2 us (9%)
  local copies, waits for them, and re-layouts  9.61 us (8%)
  Pallas kernels  9.28 us (8%)
    all_to_all x1, blocking collectives, body(): lax.all_to_all(send.reshape(32, 32, 128), ('zh', 'yl', 'yh', 'c'), 0, 0,...  25.7 us
    ppermute x8, starting transfers between devices, exchange(): return lax.ppermute(block, NAMES, step_pairs(axis, step))  22.8 us
    all_to_all x1, blocking collectives, body(): parts = lax.all_to_all(partial.reshape(8, 64, 512), FEAT, 0, 0, tiled=True)  22.5 us
    all_to_all x1, blocking collectives, body(): raw = lax.all_to_all(query_grads, FEAT, 0, 0, tiled=True)  18.1 us
    ppermute x8, waiting for transfers between devices, exchange(): return lax.ppermute(block, NAMES, step_pairs(axis, step))  11.2 us
    unnamed x19, local copies, waits for them, and re-layouts  8.7 us
    pallas_call x1, Pallas kernels, late_scores(): pl.pallas_call(late_kernel, out_shape=jax.ShapeDtypeStruct((32, 16, 512),...  4.13 us
    pallas_call x1, Pallas kernels, early_scores(): pl.pallas_call(early_kernel, out_shape=jax.ShapeDtypeStruct((256, 512), j...  2.9 us
  transfers between devices with their start and end apart: 8, of which 5 were waited for; matrix products, arithmetic and copies ran while one was open for 6% of the time, Pallas kernels for 2%

profile of v1, /device:TPU:1, one launch (start us, length us, event | category | flops | bytes accessed | tf_op | source)
XLA Modules:
  0.0 119.7 jit_solution(12324017839963113340)
XLA Ops:
  0.0 18.1 %all_to_all.15.q_ref = bf16[8,2,16,128]{3,2,1,0:T(8,128)(2,1)} all-to-all(bf16[8,2,16,128]{3,2,1,0:T(8,128)(2,1)} %param.7), channel_id=1, replica_groups=mesh['zh'=2,'zl'=4,'yl'=2,'x'=4,'yh'=4,'c'=2] {'yh','c'}, dimensions={0} | all-to-all | bytes 131072 | tf_op jit(solution)/shard_map/all_to_all | solution.py:114
  18.1 2.2 %shard_map.64 = bf16[4,8,2,16,128]{4,3,2,1,0:T(8,128)(2,1)} custom-call(bf16[8,2,16,128]{3,2,1,0:T(8,128)(2,1)} %all_to_all.15.q_ref, f32[2,128,128]{2,1,0:T(8,128)} %out_inv_ref.1, f32[2,128,128]{2,1,0:T(8,128)} %in_inv_ref.1), custom_call_target="tpu_custom_call" | custom-call | flops 200000000 | bytes 700000 | tf_op jit(solution)/shard_map/pallas_call | solution.py:68
  20.3 25.7 %all_to_all.16 = bf16[32,32,128]{2,1,0:T(8,128)(2,1)S(1)} all-to-all(bf16[32,32,128]{2,1,0:T(8,128)(2,1)} %bitcast.40), channel_id=1, replica_groups=mesh['zh'=2,'zl'=4,'yl'=2,'x'=4,'yh'=4,'c'=2] {'zh','yl','yh','c'}, dimensions={0} | all-to-all | bytes 524288 | tf_op jit(solution)/shard_map/all_to_all | solution.py:116
  46.0 0.1 copy.19
  46.1 2.4 %collective-permute-start.3 = (bf16[16,4096]{1,0:T(8,128)(2,1)S(1)}, bf16[16,4096]{1,0:T(8,128)(2,1)S(1)}, u32[]{:S(2)}, u32[]{:S(2)}) collective-permute-start(bf16[16,4096]{1,0:T(8,128)(2,1)S(1)} %bitcast.36), channel_id=1, source_target_pairs={{0,64},{1,449},{2,66},{3,451},{4,68},{5,453},{6,70},{7,455},{8,72}... | collective-permute-start | bytes 393224 | tf_op jit(solution)/shard_map/ppermute | solution.py:50
  48.6 0.1 copy.20
  48.6 4.4 %collective-permute-start = (bf16[16,4096]{1,0:T(8,128)(2,1)S(1)}, bf16[16,4096]{1,0:T(8,128)(2,1)S(1)}, u32[]{:S(2)}, u32[]{:S(2)}) collective-permute-start(bf16[16,4096]{1,0:T(8,128)(2,1)S(1)} %bitcast.33), channel_id=1, source_target_pairs={{0,8},{1,25},{2,10},{3,27},{4,12},{5,29},{6,14},{7,31},{8,0},{9,17... | collective-permute-start | bytes 393224 | tf_op jit(solution)/shard_map/ppermute | solution.py:50
  53.0 0.3 collective-permute-done.3
  53.3 3.8 %collective-permute-start.4 = (bf16[32,4096]{1,0:T(8,128)(2,1)S(1)}, bf16[32,4096]{1,0:T(8,128)(2,1)S(1)}, u32[]{:S(2)}, u32[]{:S(2)}) collective-permute-start(bf16[32,4096]{1,0:T(8,128)(2,1)S(1)} %pad_maximum_fusion.3), channel_id=1, source_target_pairs={{0,448},{1,65},{2,450},{3,67},{4,452},{5,69},{6,454},{7,71},{8,456... | collective-permute-start | bytes 786440 | tf_op jit(solution)/shard_map/ppermute | solution.py:50
  57.2 1.9 %collective-permute-start.1 = (bf16[32,4096]{1,0:T(8,128)(2,1)S(1)}, bf16[32,4096]{1,0:T(8,128)(2,1)S(1)}, u32[]{:S(2)}, u32[]{:S(2)}) collective-permute-start(bf16[32,4096]{1,0:T(8,128)(2,1)S(1)} %pad_maximum_fusion.2), channel_id=1, source_target_pairs={{0,24},{1,9},{2,26},{3,11},{4,28},{5,13},{6,30},{7,15},{8,16},{9,1... | collective-permute-start | bytes 786440 | tf_op jit(solution)/shard_map/ppermute | solution.py:50
  59.2 1.8 %collective-permute-done.4 = bf16[32,4096]{1,0:T(8,128)(2,1)S(1)} collective-permute-done((bf16[32,4096]{1,0:T(8,128)(2,1)S(1)}, bf16[32,4096]{1,0:T(8,128)(2,1)S(1)}, u32[]{:S(2)}, u32[]{:S(2)}) %collective-permute-start.4) | collective-permute-done | bytes 262176 | tf_op jit(solution)/shard_map/ppermute | solution.py:50
  61.0 4.2 %collective-permute-start.5 = (bf16[64,4096]{1,0:T(8,128)(2,1)S(1)}, bf16[64,4096]{1,0:T(8,128)(2,1)S(1)}, u32[]{:S(2)}, u32[]{:S(2)}) collective-permute-start(bf16[64,4096]{1,0:T(8,128)(2,1)S(1)} %pad_maximum_fusion.1), channel_id=1, source_target_pairs={{0,8},{1,25},{2,10},{3,27},{4,12},{5,29},{6,14},{7,31},{8,0},{9,17... | collective-permute-start | bytes 1572872 | tf_op jit(solution)/shard_map/ppermute | solution.py:50
  65.3 2.2 %collective-permute-start.2 = (bf16[64,4096]{1,0:T(8,128)(2,1)S(1)}, bf16[64,4096]{1,0:T(8,128)(2,1)S(1)}, u32[]{:S(2)}, u32[]{:S(2)}) collective-permute-start(bf16[64,4096]{1,0:T(8,128)(2,1)S(1)} %pad_maximum_fusion), channel_id=1, source_target_pairs={{0,64},{1,449},{2,66},{3,451},{4,68},{5,453},{6,70},{7,455},{8,72}... | collective-permute-start | bytes 1572872 | tf_op jit(solution)/shard_map/ppermute | solution.py:50
  67.5 4.6 %collective-permute-done.5 = bf16[64,4096]{1,0:T(8,128)(2,1)S(1)} collective-permute-done((bf16[64,4096]{1,0:T(8,128)(2,1)S(1)}, bf16[64,4096]{1,0:T(8,128)(2,1)S(1)}, u32[]{:S(2)}, u32[]{:S(2)}) %collective-permute-start.5) | collective-permute-done | bytes 524320 | tf_op jit(solution)/shard_map/ppermute | solution.py:50
  72.2 2.0 %collective-permute-start.7 = (bf16[128,4096]{1,0:T(8,128)(2,1)S(1)}, bf16[128,4096]{1,0:T(8,128)(2,1)S(1)}, u32[]{:S(2)}, u32[]{:S(2)}) collective-permute-start(bf16[128,4096]{1,0:T(8,128)(2,1)S(1)} %constant_dynamic-update-slice_fusion.4.pre_b_ref), channel_id=1, source_target_pairs={{0,24},{1,9},{2,26},{3,11},{4,28},{5,13},{6,30},{7,15},{8,16},{9,1... | collective-permute-start | bytes 3145736 | tf_op jit(solution)/shard_map/ppermute | solution.py:50
  74.2 2.2 %collective-permute-done.2 = bf16[64,4096]{1,0:T(8,128)(2,1)S(1)} collective-permute-done((bf16[64,4096]{1,0:T(8,128)(2,1)S(1)}, bf16[64,4096]{1,0:T(8,128)(2,1)S(1)}, u32[]{:S(2)}, u32[]{:S(2)}) %collective-permute-start.2) | collective-permute-done | bytes 524320 | tf_op jit(solution)/shard_map/ppermute | solution.py:50
  76.4 1.9 %collective-permute-start.6 = (bf16[128,4096]{1,0:T(8,128)(2,1)S(1)}, bf16[128,4096]{1,0:T(8,128)(2,1)}, u32[]{:S(2)}, u32[]{:S(2)}) collective-permute-start(bf16[128,4096]{1,0:T(8,128)(2,1)S(1)} %constant_dynamic-update-slice_fusion.pre_a_ref), channel_id=1, source_target_pairs={{0,448},{1,65},{2,450},{3,67},{4,452},{5,69},{6,454},{7,71},{8,456... | collective-permute-start | bytes 3145736 | tf_op jit(solution)/shard_map/ppermute | solution.py:50
  78.4 0.0 copy-start.3
  78.4 0.0 copy-start.4
  78.4 6.2 %copy.18 = bf16[64,8,32,128]{3,1,2,0:T(8,128)(2,1)} copy(bf16[64,8,32,128]{3,2,1,0:T(8,128)(2,1)S(1)} %bitcast.28) | data formatting | bytes 8388608
  84.6 0.1 broadcast_add_fusion.1
  84.7 0.1 add.41
  84.8 0.1 add.46
  84.9 0.1 pad_add_fusion.place_ref
  84.9 2.2 %copy-done = bf16[64,8,32,128]{3,1,2,0:T(8,128)(2,1)S(1)} copy-done((bf16[64,8,32,128]{3,1,2,0:T(8,128)(2,1)S(1)}, bf16[64,8,32,128]{3,1,2,0:T(8,128)(2,1)}, u32[]{:S(2)}) %copy-start) | copy-done | bytes 4194328
  87.1 2.9 %shard_map.65.early_ref = bf16[256,512]{1,0:T(8,128)(2,1)S(1)} custom-call(bf16[128,4096]{1,0:T(8,128)(2,1)S(1)} %constant_dynamic-update-slice_fusion.pre_a_ref, bf16[128,4096]{1,0:T(8,128)(2,1)S(1)} %constant_dynamic-update-slice_fusion.4.pre_b_ref, bf16[512,4096]{1,0:T(8,128)(2,1)S(1)} %bitcast.25), custom_call_target="tpu_custom_call" | custom-call | flops 1073741824 | bytes 7000000 | tf_op jit(solution)/shard_map/pallas_call | solution.py:93
  90.0 0.0 collective-permute-done.7.pre_b_ref
  90.1 2.3 %collective-permute-done.6.pre_a_ref = bf16[128,4096]{1,0:T(8,128)(2,1)} collective-permute-done((bf16[128,4096]{1,0:T(8,128)(2,1)S(1)}, bf16[128,4096]{1,0:T(8,128)(2,1)}, u32[]{:S(2)}, u32[]{:S(2)}) %collective-permute-start.6) | collective-permute-done | bytes 1048608 | tf_op jit(solution)/shard_map/ppermute | solution.py:50
  92.4 4.1 %shard_map.66 = bf16[32,16,512]{2,1,0:T(8,128)(2,1)S(1)} custom-call(s32[32]{0:T(128)S(1)} %pad_add_fusion.place_ref, bf16[256,512]{1,0:T(8,128)(2,1)S(1)} %shard_map.65.early_ref, bf16[128,4096]{1,0:T(8,128)(2,1)} %collective-permute-done.6.pre_a_ref, bf16[128,4096]{1,0:T(8,128)(2,1)S(1)} %collective-permute-done.7.pre_b_ref, bf16[512,4096]{1,0:T(8,128)(2,1)S(1)} %bitcast.26), custom_call_target="tpu_custom_call" | custom-call | flops 1073741824 | bytes 7000000 | tf_op jit(solution)/shard_map/pallas_call | solution.py:103
  96.5 22.5 %all_to_all.17 = bf16[8,64,512]{2,1,0:T(8,128)(2,1)S(1)} all-to-all(bf16[8,64,512]{2,1,0:T(8,128)(2,1)S(1)} %bitcast.27), channel_id=1, replica_groups=mesh['zh'=2,'zl'=4,'yl'=2,'x'=4,'yh'=4,'c'=2] {'yh','c'}, dimensions={0} | all-to-all | bytes 1048576 | tf_op jit(solution)/shard_map/all_to_all | solution.py:138
  119.0 0.1 convert_reduce_fusion
  119.1 0.7 copy.7
  (23 shorter events, 0.4 us)
Async XLA Ops:
  46.0 32.4 %copy-start.2 = (bf16[512,2,16,128]{3,2,1,0:T(8,128)(2,1)S(1)}, bf16[512,2,16,128]{3,2,1,0:T(8,128)(2,1)}, u32[]{:S(2)}) copy-start(bf16[512,2,16,128]{3,2,1,0:T(8,128)(2,1)} %param.6) | copy-start | bytes 12582916
  46.1 7.2 %collective-permute-start.3 = (bf16[16,4096]{1,0:T(8,128)(2,1)S(1)}, bf16[16,4096]{1,0:T(8,128)(2,1)S(1)}, u32[]{:S(2)}, u32[]{:S(2)}) collective-permute-start(bf16[16,4096]{1,0:T(8,128)(2,1)S(1)} %bitcast.36), channel_id=1, source_target_pairs={{0,64},{1,449},{2,66},{3,451},{4,68},{5,453},{6,70},{7,455},{8,72}... | collective-permute-start | bytes 393224 | tf_op jit(solution)/shard_map/ppermute | solution.py:50
  48.6 8.5 %collective-permute-start = (bf16[16,4096]{1,0:T(8,128)(2,1)S(1)}, bf16[16,4096]{1,0:T(8,128)(2,1)S(1)}, u32[]{:S(2)}, u32[]{:S(2)}) collective-permute-start(bf16[16,4096]{1,0:T(8,128)(2,1)S(1)} %bitcast.33), channel_id=1, source_target_pairs={{0,8},{1,25},{2,10},{3,27},{4,12},{5,29},{6,14},{7,31},{8,0},{9,17... | collective-permute-start | bytes 393224 | tf_op jit(solution)/shard_map/ppermute | solution.py:50
  53.3 7.6 %collective-permute-start.4 = (bf16[32,4096]{1,0:T(8,128)(2,1)S(1)}, bf16[32,4096]{1,0:T(8,128)(2,1)S(1)}, u32[]{:S(2)}, u32[]{:S(2)}) collective-permute-start(bf16[32,4096]{1,0:T(8,128)(2,1)S(1)} %pad_maximum_fusion.3), channel_id=1, source_target_pairs={{0,448},{1,65},{2,450},{3,67},{4,452},{5,69},{6,454},{7,71},{8,456... | collective-permute-start | bytes 786440 | tf_op jit(solution)/shard_map/ppermute | solution.py:50
  57.2 8.0 %collective-permute-start.1 = (bf16[32,4096]{1,0:T(8,128)(2,1)S(1)}, bf16[32,4096]{1,0:T(8,128)(2,1)S(1)}, u32[]{:S(2)}, u32[]{:S(2)}) collective-permute-start(bf16[32,4096]{1,0:T(8,128)(2,1)S(1)} %pad_maximum_fusion.2), channel_id=1, source_target_pairs={{0,24},{1,9},{2,26},{3,11},{4,28},{5,13},{6,30},{7,15},{8,16},{9,1... | collective-permute-start | bytes 786440 | tf_op jit(solution)/shard_map/ppermute | solution.py:50
  61.0 11.1 %collective-permute-start.5 = (bf16[64,4096]{1,0:T(8,128)(2,1)S(1)}, bf16[64,4096]{1,0:T(8,128)(2,1)S(1)}, u32[]{:S(2)}, u32[]{:S(2)}) collective-permute-start(bf16[64,4096]{1,0:T(8,128)(2,1)S(1)} %pad_maximum_fusion.1), channel_id=1, source_target_pairs={{0,8},{1,25},{2,10},{3,27},{4,12},{5,29},{6,14},{7,31},{8,0},{9,17... | collective-permute-start | bytes 1572872 | tf_op jit(solution)/shard_map/ppermute | solution.py:50
  65.3 11.1 %collective-permute-start.2 = (bf16[64,4096]{1,0:T(8,128)(2,1)S(1)}, bf16[64,4096]{1,0:T(8,128)(2,1)S(1)}, u32[]{:S(2)}, u32[]{:S(2)}) collective-permute-start(bf16[64,4096]{1,0:T(8,128)(2,1)S(1)} %pad_maximum_fusion), channel_id=1, source_target_pairs={{0,64},{1,449},{2,66},{3,451},{4,68},{5,453},{6,70},{7,455},{8,72}... | collective-permute-start | bytes 1572872 | tf_op jit(solution)/shard_map/ppermute | solution.py:50
  72.2 17.9 %collective-permute-start.7 = (bf16[128,4096]{1,0:T(8,128)(2,1)S(1)}, bf16[128,4096]{1,0:T(8,128)(2,1)S(1)}, u32[]{:S(2)}, u32[]{:S(2)}) collective-permute-start(bf16[128,4096]{1,0:T(8,128)(2,1)S(1)} %constant_dynamic-update-slice_fusion.4.pre_b_ref), channel_id=1, source_target_pairs={{0,24},{1,9},{2,26},{3,11},{4,28},{5,13},{6,30},{7,15},{8,16},{9,1... | collective-permute-start | bytes 3145736 | tf_op jit(solution)/shard_map/ppermute | solution.py:50
  76.4 15.9 %collective-permute-start.6 = (bf16[128,4096]{1,0:T(8,128)(2,1)S(1)}, bf16[128,4096]{1,0:T(8,128)(2,1)}, u32[]{:S(2)}, u32[]{:S(2)}) collective-permute-start(bf16[128,4096]{1,0:T(8,128)(2,1)S(1)} %constant_dynamic-update-slice_fusion.pre_a_ref), channel_id=1, source_target_pairs={{0,448},{1,65},{2,450},{3,67},{4,452},{5,69},{6,454},{7,71},{8,456... | collective-permute-start | bytes 3145736 | tf_op jit(solution)/shard_map/ppermute | solution.py:50
  78.4 6.2 %copy-start.3 = (s32[4]{0:T(128)S(1)}, s32[4]{0:T(128)}, u32[]{:S(2)}) copy-start(s32[4]{0:T(128)} %constant.26.clone) | copy-start | bytes 52
  78.4 6.2 %copy-start.4 = (s32[4]{0:T(128)S(1)}, s32[4]{0:T(128)}, u32[]{:S(2)}) copy-start(s32[4]{0:T(128)} %constant.27.clone) | copy-start | bytes 52
  84.9 2.2 %copy-start = (bf16[64,8,32,128]{3,1,2,0:T(8,128)(2,1)S(1)}, bf16[64,8,32,128]{3,1,2,0:T(8,128)(2,1)}, u32[]{:S(2)}) copy-start(bf16[64,8,32,128]{3,1,2,0:T(8,128)(2,1)} %copy.18) | copy-start | bytes 12582916
  87.1 5.2 %copy-start.1 = (bf16[64,8,32,128]{3,1,2,0:T(8,128)(2,1)S(1)}, bf16[64,8,32,128]{3,1,2,0:T(8,128)(2,1)}, u32[]{:S(2)}) copy-start(bf16[64,8,32,128]{3,1,2,0:T(8,128)(2,1)} %copy.18) | copy-start | bytes 12582916

commit v2 on v0

v2 whole, which is shorter than its diff:
```python
import jax
import jax.numpy as jnp
from jax import lax
from jax.experimental import pallas as pl
from jax.experimental.pallas import tpu as pltpu
from jax.sharding import Mesh
from jax.sharding import PartitionSpec as P

NAMES = ("zh", "zl", "yl", "x", "yh", "c")
SIZES = (2, 4, 2, 4, 4, 2)
WHOLE = pl.BlockSpec(memory_space=pltpu.VMEM)
BIG = pltpu.CompilerParams(vmem_limit_bytes=24 * 1024 * 1024)
SMALL = pltpu.CompilerParams(vmem_limit_bytes=12 * 1024 * 1024)


def near(core):
    return (1, 3) if core == 0 else (3, 1)


def device_index(zh, zl, yl, x, yh, c):
    index = 0
    for size, at in zip(SIZES, (zh, zl, yl, x, yh, c)):
        index = index * size + at
    return index


def step_pairs(step, along_x, along_z):
    pairs = []
    for z in range(8):
        for yl in range(2):
            for x in range(4):
                for yh in range(4):
                    for c in range(2):
                        mask = near(c)[step]
                        z2, x2 = z, x
                        if along_x:
                            x2 = x ^ mask
                        if along_z:
                            z2 = z ^ 1 if mask == 1 else (z + (1 if z % 2 else -1)) % 8
                        pairs.append(
                            (
                                device_index(z // 4, z % 4, yl, x, yh, c),
                                device_index(z2 // 4, z2 % 4, yl, x2, yh, c),
                            )
                        )
    return pairs


def exchange(block, step, along_x, along_z):
    return lax.ppermute(block, NAMES, step_pairs(step, along_x, along_z))


def three_parts(value):
    top = value.astype(jnp.bfloat16)
    rest = value - top.astype(jnp.float32)
    middle = rest.astype(jnp.bfloat16)
    low = (rest - middle.astype(jnp.float32)).astype(jnp.bfloat16)
    return jnp.concatenate([top, middle, low])


def precond_kernel(raw_ref, out_inv_ref, in_inv_ref, pre_ref):
    feat = lax.axis_index("yh") * 2 + lax.axis_index("c")
    for layer in range(2):
        own = three_parts(out_inv_ref[layer, pl.ds(feat * 16, 16), :])
        mixed = []
        for q in range(8):
            whole = jnp.concatenate([raw_ref[f % 2, f // 2, q, layer] for f in range(8)])
            parts = jnp.dot(own, whole, preferred_element_type=jnp.float32)
            mixed.append((parts[32:] + parts[16:32]) + parts[:16])
        rows = jnp.dot(
            jnp.concatenate(mixed),
            in_inv_ref[layer],
            precision=lax.Precision.HIGHEST,
            preferred_element_type=jnp.float32,
        )
        rows = rows.astype(jnp.bfloat16).reshape(8, 16, 128)
        for copy in range(4):
            pre_ref[copy, :, layer] = rows


def precondition(raw, out_inv, in_inv):
    return pl.pallas_call(
        precond_kernel,
        out_shape=jax.ShapeDtypeStruct((4, 8, 2, 16, 128), jnp.bfloat16),
        in_specs=[WHOLE] * 3,
        out_specs=WHOLE,
        cost_estimate=pl.CostEstimate(flops=100_000_000, bytes_accessed=1_000_000, transcendentals=0),
        compiler_params=SMALL,
    )(raw, out_inv, in_inv)


def nt_dot(a, b):
    return lax.dot_general(a, b, (((1,), (1,)), ((), ())), preferred_element_type=jnp.float32)


def z_side(core):
    return (lax.axis_index("zl") & 1) ^ core


def split_rows(half, scores, keep_ref, send_ref):
    side = z_side(lax.axis_index("c"))
    mine = side if half == 0 else 1 - side
    for piece in range(2):
        keep_ref[piece * 64 : piece * 64 + 64] = scores[pl.ds(pl.multiple_of(piece * 128 + mine * 64, 64), 64), :]
        send_ref[piece * 64 : piece * 64 + 64] = scores[pl.ds(pl.multiple_of(piece * 128 + 64 - mine * 64, 64), 64), :]


def early_kernel(pre_0_ref, pre_1a_ref, pre_1b_ref, train_ref, keep_ref, send_ref, scores):
    pre = jnp.concatenate([pre_0_ref[...], pre_1a_ref[...], pre_1b_ref[...]])
    scores[...] = nt_dot(pre, train_ref[...])
    split_rows(0, scores, keep_ref, send_ref)


def middle_kernel(pre_a_ref, pre_b_ref, train_ref, scores_ref):
    scores_ref[...] = nt_dot(jnp.concatenate([pre_a_ref[...], pre_b_ref[...]]), train_ref[...])


def late_kernel(middle_ref, pre_a_ref, pre_b_ref, train_ref, keep_ref, send_ref, scores):
    scores[:128] = middle_ref[...]
    scores[128:] = nt_dot(jnp.concatenate([pre_a_ref[...], pre_b_ref[...]]), train_ref[...])
    split_rows(1, scores, keep_ref, send_ref)


def score_call(kernel, queries, *operands):
    half = jax.ShapeDtypeStruct((128, 512), jnp.float32)
    split = kernel is not middle_kernel
    return pl.pallas_call(
        kernel,
        out_shape=(half, half) if split else half,
        in_specs=[WHOLE] * len(operands),
        out_specs=(WHOLE, WHOLE) if split else WHOLE,
        scratch_shapes=[pltpu.VMEM((256, 512), jnp.float32)] if split else [],
        cost_estimate=pl.CostEstimate(
            flops=queries * 512 * 4096 * 2, bytes_accessed=queries * 8192 + 4_194_304, transcendentals=0
        ),
        compiler_params=BIG,
    )(*operands)


def block_places(half, core):
    x, zl = lax.axis_index("x"), lax.axis_index("zl")
    side = z_side(lax.axis_index("c"))
    first = jnp.where(core == 0, 1, 3)
    second = jnp.where(core == 0, 3, 1)
    mask_z = jnp.where(side == 0, 0 if half == 0 else 2, first if half == 0 else second)
    z1 = (zl ^ mask_z) >> 1
    places = []
    for of_piece in (0, second):
        for of_slot in (0, first):
            for zh in range(2):
                places.append((2 * zh + z1) * 4 + (x ^ of_piece ^ of_slot))
    return places


def combine_kernel(keep_0_ref, keep_1_ref, got_0_ref, got_1_ref, out_ref, total):
    core = lax.axis_index("c")
    for half, keep_ref in enumerate((keep_0_ref, keep_1_ref)):
        for block, place in enumerate(block_places(half, core)):
            total[place] = keep_ref[block * 16 : block * 16 + 16]
    for half, got_ref in enumerate((got_0_ref, got_1_ref)):
        for block, place in enumerate(block_places(half, 1 - core)):
            total[place] = total[place] + got_ref[1 - core, block * 16 : block * 16 + 16]
    out_ref[...] = total[...].astype(jnp.bfloat16)


def combine(keeps, gots):
    return pl.pallas_call(
        combine_kernel,
        out_shape=jax.ShapeDtypeStruct((16, 16, 512), jnp.bfloat16),
        in_specs=[WHOLE] * 4,
        out_specs=WHOLE,
        scratch_shapes=[pltpu.VMEM((16, 16, 512), jnp.float32)],
        cost_estimate=pl.CostEstimate(flops=262_144, bytes_accessed=2_000_000, transcendentals=0),
        compiler_params=SMALL,
    )(*keeps, *gots)


def sum_kernel(parts_ref, out_ref):
    for x in range(4):
        total = parts_ref[0, x].astype(jnp.float32)
        for chip in range(1, 4):
            total = total + parts_ref[chip, x].astype(jnp.float32)
        out_ref[x * 8 : x * 8 + 8] = total[:8]
        out_ref[32 + x * 8 : 40 + x * 8] = total[8:]


def final_sum(parts):
    return pl.pallas_call(
        sum_kernel,
        out_shape=jax.ShapeDtypeStruct((64, 512), jnp.float32),
        in_specs=[WHOLE],
        out_specs=WHOLE,
        cost_estimate=pl.CostEstimate(flops=131_072, bytes_accessed=400_000, transcendentals=0),
        compiler_params=SMALL,
    )(parts)


def body(train_grads, query_grads, out_inv, in_inv):
    copies = jnp.broadcast_to(query_grads[None], (4,) + query_grads.shape)
    raw = lax.all_gather(lax.all_to_all(copies, "yh", 0, 0, tiled=True), "c")
    pre = precondition(raw, out_inv, in_inv).reshape(4, 8, 32, 128)
    pre = lax.all_to_all(pre, ("zh", "yl"), 0, 0, tiled=True)
    held = pre.reshape(32, 4096)
    train = train_grads.reshape(512, 4096)
    along_x, along_z, along_both = (True, False), (False, True), (True, True)
    square = jnp.concatenate([held] + [exchange(held, 0, *way) for way in (along_x, along_z, along_both)])
    square, train = lax.optimization_barrier((square, train))
    first, second = square[:64], square[64:]
    x_first, z_second = exchange(first, 1, *along_x), exchange(second, 1, *along_z)
    x_second, z_first = exchange(second, 1, *along_x), exchange(first, 1, *along_z)
    both_first, both_second = exchange(x_first, 1, *along_z), exchange(z_second, 1, *along_x)

    keep_0, send_0 = score_call(early_kernel, 256, square, x_first, x_second, train)
    got_0 = lax.all_gather(send_0, "c")
    middle = score_call(middle_kernel, 128, z_first, z_second, train)
    keep_1, send_1 = score_call(late_kernel, 128, middle, both_first, both_second, train)
    got_1 = lax.all_gather(send_1, "c")
    chip_sum = combine((keep_0, keep_1), (got_0, got_1))
    parts = lax.all_to_all(chip_sum.reshape(4, 4, 16, 512), "yh", 0, 0, tiled=True)
    return final_sum(parts).T


def solution(mesh):
    fine = Mesh(mesh.devices.reshape(SIZES), NAMES)
    rows, feat = ("zh", "zl", "yl", "x"), ("yh", "c")
    placed = (P(rows, None, feat, None), P(rows, None, feat, None), P(), P())
    return jax.shard_map(
        body, mesh=fine, in_specs=placed, out_specs=P(rows, feat), check_vma=False
    )
```

time: 350 us -> 110 us (0.31)
  waiting for transfers between devices: 323 us -> 1.87 us
  blocking collectives: 0 us -> 63.5 us
  starting transfers between devices: 0.09 us -> 28 us
  between operations: 13.1 us -> 0.2 us
  matrix products: 11.1 us -> 0 us
  local copies, waits for them, and re-layouts: 1.55 us -> 9.23 us
  Pallas kernels: 0 us -> 5.9 us
    all_gather x2 -> x0, waiting for transfers between devices: 252 us -> none  [the longest x1 213 us: body(): piece = lax.all_gather(precond, 'rows', axis=0, tiled=True)]
    reduce_scatter x1 -> x0, waiting for transfers between devices: 71.2 us -> none  [body(): lax.psum_scatter(partial_scores, 'feat', scatter_dimension=1, tiled=True)]
    all_to_all x0 -> x3, blocking collectives: none -> 47 us  [the longest x1 18.8 us: body(): pre = lax.all_to_all(pre, ('zh', 'yl'), 0, 0, tiled=True)]
    ppermute x0 -> x9, starting transfers between devices: none -> 28 us  [exchange(): return lax.ppermute(block, NAMES, step_pairs(step, along_x, along_z))]
    all_gather x0 -> x3, blocking collectives: none -> 16.5 us  [the longest x1 7.7 us: body(): got_0 = lax.all_gather(send_0, 'c')]
    dot_general x3 -> x0, matrix products: 11.1 us -> none  [the longest x1 7.3 us: body(): lax.dot_general(train_flat, flat_piece, (((1,), (1,)), ((), ())), preferr...]
    unnamed x2 -> x5, local copies, waits for them, and re-layouts: 0.9 us -> 8.16 us
    pallas_call x0 -> x6, Pallas kernels: none -> 5.9 us  [the longest x3 4.39 us: score_call(): pl.pallas_call(kernel, out_shape=(half, half) if split else half, in_spec...]
  transfers between devices with their start and end apart: 3 -> 9, of which waited for: 3 -> 1; matrix products, arithmetic and copies ran while one was open for 0% -> 6% of each run, Pallas kernels for 0% -> 3%
where the time goes in v2:
time: 110 us; the launch traced here: 109 us
  blocking collectives  63.5 us (58%)
  starting transfers between devices  28 us (25%)
  local copies, waits for them, and re-layouts  9.23 us (8%)
  Pallas kernels  5.9 us (5%)
  waiting for transfers between devices  1.87 us (2%)
    ppermute x9, starting transfers between devices, exchange(): return lax.ppermute(block, NAMES, step_pairs(step, along_x, along_z))  28 us
    all_to_all x1, blocking collectives, body(): pre = lax.all_to_all(pre, ('zh', 'yl'), 0, 0, tiled=True)  18.8 us
    all_to_all x1, blocking collectives, body(): raw = lax.all_gather(lax.all_to_all(copies, 'yh', 0, 0, tiled=True), 'c')  16.4 us
    all_to_all x1, blocking collectives, body(): lax.all_to_all(chip_sum.reshape(4, 4, 16, 512), 'yh', 0, 0, tiled=True)  11.8 us
    unnamed x5, local copies, waits for them, and re-layouts  8.16 us
    all_gather x1, blocking collectives, body(): got_0 = lax.all_gather(send_0, 'c')  7.7 us
    all_gather x1, blocking collectives, body(): raw = lax.all_gather(lax.all_to_all(copies, 'yh', 0, 0, tiled=True), 'c')  4.59 us
    pallas_call x3, Pallas kernels, score_call(): pl.pallas_call(kernel, out_shape=(half, half) if split else half, in_spec...  4.39 us
  transfers between devices with their start and end apart: 9, of which 1 were waited for; matrix products, arithmetic and copies ran while one was open for 6% of the time, Pallas kernels for 3%

profile of v2, /device:TPU:1, one launch (start us, length us, event | category | flops | bytes accessed | tf_op | source)
XLA Modules:
  0.0 108.8 jit_solution(11694428518319525737)
XLA Ops:
  0.0 0.9 broadcast_in_dim.2
  0.9 16.4 %all_to_all.15 = bf16[4,8,2,16,128]{4,3,2,1,0:T(8,128)(2,1)S(1)} all-to-all(bf16[4,8,2,16,128]{4,3,2,1,0:T(8,128)(2,1)S(1)} %broadcast_in_dim.2), channel_id=1, replica_groups=mesh['zh'=2,'zl'=4,'yl'=2,'x'=4,'yh'=4,'c'=2] {'yh'}, dimensions={0} | all-to-all | bytes 524288 | tf_op jit(solution)/shard_map/all_to_all | solution.py:200
  17.3 4.6 %all-gather = bf16[8,8,2,16,128]{4,3,2,1,0:T(8,128)(2,1)S(1)} all-gather(bf16[4,8,2,16,128]{4,3,2,1,0:T(8,128)(2,1)S(1)} %all_to_all.15), channel_id=2, replica_groups=mesh['zh'=2,'zl'=4,'yl'=2,'x'=4,'yh'=4,'c'=2] {'c'}, dimensions={0}, use_global_device_ids=true | all-gather | bytes 786432 | tf_op jit(solution)/shard_map/all_gather | solution.py:200
  21.9 0.9 copy-done
  22.8 0.9 copy-done.1
  23.7 0.7 shard_map.46
  24.4 0.1 copy.6
  24.5 18.8 %all_to_all.16 = bf16[4,8,32,128]{3,1,2,0:T(8,128)(2,1)S(1)} all-to-all(bf16[4,8,32,128]{3,1,2,0:T(8,128)(2,1)S(1)} %copy.6), channel_id=1, replica_groups=mesh['zh'=2,'zl'=4,'yl'=2,'x'=4,'yh'=4,'c'=2] {'zh','yl'}, dimensions={0} | all-to-all | bytes 524288 | tf_op jit(solution)/shard_map/all_to_all | solution.py:202
  43.3 5.0 %collective-permute-start.2 = (bf16[32,4096]{1,0:T(8,128)(2,1)S(1)}, bf16[32,4096]{1,0:T(8,128)(2,1)S(1)}, u32[]{:S(2)}, u32[]{:S(2)}) collective-permute-start(bf16[32,4096]{1,0:T(8,128)(2,1)S(1)} %bitcast.21), channel_id=1, source_target_pairs={{0,72},{1,473},{2,74},{3,475},{4,76},{5,477},{6,78},{7,479},{8,64}... | collective-permute-start | bytes 786440 | tf_op jit(solution)/shard_map/ppermute | solution.py:50
  48.3 3.7 %collective-permute-start.1 = (bf16[32,4096]{1,0:T(8,128)(2,1)S(1)}, bf16[32,4096]{1,0:T(8,128)(2,1)S(1)}, u32[]{:S(2)}, u32[]{:S(2)}) collective-permute-start(bf16[32,4096]{1,0:T(8,128)(2,1)S(1)} %bitcast.22), channel_id=1, source_target_pairs={{0,64},{1,449},{2,66},{3,451},{4,68},{5,453},{6,70},{7,455},{8,72}... | collective-permute-start | bytes 786440 | tf_op jit(solution)/shard_map/ppermute | solution.py:50
  52.0 2.1 %collective-permute-start = (bf16[32,4096]{1,0:T(8,128)(2,1)S(1)}, bf16[32,4096]{1,0:T(8,128)(2,1)S(1)}, u32[]{:S(2)}, u32[]{:S(2)}) collective-permute-start(bf16[32,4096]{1,0:T(8,128)(2,1)S(1)} %bitcast.23), channel_id=1, source_target_pairs={{0,8},{1,25},{2,10},{3,27},{4,12},{5,29},{6,14},{7,31},{8,0},{9,17... | collective-permute-start | bytes 786440 | tf_op jit(solution)/shard_map/ppermute | solution.py:50
  54.1 6.4 %copy.9 = bf16[64,8,32,128]{3,1,2,0:T(8,128)(2,1)S(1)} copy(bf16[64,8,32,128]{3,2,1,0:T(8,128)(2,1)} %bitcast.20) | data formatting | bytes 8388608
  60.5 0.0 collective-permute-done.1
  60.5 0.0 collective-permute-done
  60.5 0.1 pad_maximum_fusion.pre_0_ref
  60.6 0.1 fusion
  60.7 1.9 %collective-permute-start.3 = (bf16[64,4096]{1,0:T(8,128)(2,1)S(1)}, bf16[64,4096]{1,0:T(8,128)(2,1)S(1)}, u32[]{:S(2)}, u32[]{:S(2)}) collective-permute-start(bf16[64,4096]{1,0:T(8,128)(2,1)S(1)} %get-tuple-element.18), channel_id=1, source_target_pairs={{0,24},{1,9},{2,26},{3,11},{4,28},{5,13},{6,30},{7,15},{8,16},{9,1... | collective-permute-start | bytes 1572872 | tf_op jit(solution)/shard_map/ppermute | solution.py:50
  62.6 4.7 %collective-permute-start.6 = (bf16[64,4096]{1,0:T(8,128)(2,1)S(1)}, bf16[64,4096]{1,0:T(8,128)(2,1)S(1)}, u32[]{:S(2)}, u32[]{:S(2)}) collective-permute-start(bf16[64,4096]{1,0:T(8,128)(2,1)S(1)} %get-tuple-element.17), channel_id=1, source_target_pairs={{0,448},{1,65},{2,450},{3,67},{4,452},{5,69},{6,454},{7,71},{8,456... | collective-permute-start | bytes 1572872 | tf_op jit(solution)/shard_map/ppermute | solution.py:50
  67.4 1.9 %collective-permute-start.5 = (bf16[64,4096]{1,0:T(8,128)(2,1)S(1)}, bf16[64,4096]{1,0:T(8,128)(2,1)S(1)}, u32[]{:S(2)}, u32[]{:S(2)}) collective-permute-start(bf16[64,4096]{1,0:T(8,128)(2,1)S(1)} %get-tuple-element.18), channel_id=1, source_target_pairs={{0,448},{1,65},{2,450},{3,67},{4,452},{5,69},{6,454},{7,71},{8,456... | collective-permute-start | bytes 1572872 | tf_op jit(solution)/shard_map/ppermute | solution.py:50
  69.3 3.4 %collective-permute-start.4 = (bf16[64,4096]{1,0:T(8,128)(2,1)S(1)}, bf16[64,4096]{1,0:T(8,128)(2,1)S(1)}, u32[]{:S(2)}, u32[]{:S(2)}) collective-permute-start(bf16[64,4096]{1,0:T(8,128)(2,1)S(1)} %get-tuple-element.17), channel_id=1, source_target_pairs={{0,24},{1,9},{2,26},{3,11},{4,28},{5,13},{6,30},{7,15},{8,16},{9,1... | collective-permute-start | bytes 1572872 | tf_op jit(solution)/shard_map/ppermute | solution.py:50
  72.7 0.0 collective-permute-done.3.pre_1a_ref
  72.7 3.4 %collective-permute-start.7 = (bf16[64,4096]{1,0:T(8,128)(2,1)S(1)}, bf16[64,4096]{1,0:T(8,128)(2,1)S(1)}, u32[]{:S(2)}, u32[]{:S(2)}) collective-permute-start(bf16[64,4096]{1,0:T(8,128)(2,1)S(1)} %collective-permute-done.3.pre_1a_ref), channel_id=1, source_target_pairs={{0,448},{1,65},{2,450},{3,67},{4,452},{5,69},{6,454},{7,71},{8,456... | collective-permute-start | bytes 1572872 | tf_op jit(solution)/shard_map/ppermute | solution.py:50
  76.1 1.9 %collective-permute-start.8 = (bf16[64,4096]{1,0:T(8,128)(2,1)S(1)}, bf16[64,4096]{1,0:T(8,128)(2,1)S(1)}, u32[]{:S(2)}, u32[]{:S(2)}) collective-permute-start(bf16[64,4096]{1,0:T(8,128)(2,1)S(1)} %collective-permute-done.6.pre_b_ref), channel_id=1, source_target_pairs={{0,24},{1,9},{2,26},{3,11},{4,28},{5,13},{6,30},{7,15},{8,16},{9,1... | collective-permute-start | bytes 1572872 | tf_op jit(solution)/shard_map/ppermute | solution.py:50
  78.0 1.9 %collective-permute-done.5.pre_a_ref = bf16[64,4096]{1,0:T(8,128)(2,1)S(1)} collective-permute-done((bf16[64,4096]{1,0:T(8,128)(2,1)S(1)}, bf16[64,4096]{1,0:T(8,128)(2,1)S(1)}, u32[]{:S(2)}, u32[]{:S(2)}) %collective-permute-start.5) | collective-permute-done | bytes 524320 | tf_op jit(solution)/shard_map/ppermute | solution.py:50
  79.8 1.5 %shard_map.48.middle_ref = f32[128,512]{1,0:T(8,128)S(1)} custom-call(bf16[64,4096]{1,0:T(8,128)(2,1)S(1)} %collective-permute-done.5.pre_a_ref, bf16[64,4096]{1,0:T(8,128)(2,1)S(1)} %collective-permute-done.6.pre_b_ref, bf16[512,4096]{1,0:T(8,128)(2,1)S(1)} %bitcast.12), custom_call_target="tpu_custom_call" | custom-call | flops 536870912 | bytes 5242880 | tf_op jit(solution)/shard_map/pallas_call | solution.py:127
  81.4 1.3 %shard_map.47 = (f32[128,512]{1,0:T(8,128)S(1)}, f32[128,512]{1,0:T(8,128)S(1)}) custom-call(bf16[128,4096]{1,0:T(8,128)(2,1)S(1)} %pad_maximum_fusion.pre_0_ref, bf16[64,4096]{1,0:T(8,128)(2,1)S(1)} %collective-permute-done.3.pre_1a_ref, bf16[64,4096]{1,0:T(8,128)(2,1)S(1)} %collective-permute-done.4.pre_1b_ref, bf16[512,4096]{1,0:T(8,128)(2,1)S(1)} %bitcast.13), custom_call_target="tpu_custom_call" | custom-call | flops 1073741824 | bytes 6291456 | tf_op jit(solution)/shard_map/pallas_call | solution.py:127
  82.7 7.7 %all-gather.1 = f32[256,512]{1,0:T(8,128)S(1)} all-gather(f32[128,512]{1,0:T(8,128)S(1)} %get-tuple-element.15), channel_id=3, replica_groups=mesh['zh'=2,'zl'=4,'yl'=2,'x'=4,'yh'=4,'c'=2] {'c'}, dimensions={0}, use_global_device_ids=true | all-gather | bytes 786432 | tf_op jit(solution)/shard_map/all_gather | solution.py:214
  90.4 1.6 %shard_map.49 = (f32[128,512]{1,0:T(8,128)S(1)}, f32[128,512]{1,0:T(8,128)S(1)}) custom-call(f32[128,512]{1,0:T(8,128)S(1)} %shard_map.48.middle_ref, bf16[64,4096]{1,0:T(8,128)(2,1)S(1)} %collective-permute-done.7.pre_a_ref, bf16[64,4096]{1,0:T(8,128)(2,1)S(1)} %collective-permute-done.8.pre_b_ref, bf16[512,4096]{1,0:T(8,128)(2,1)S(1)} %bitcast.14), custom_call_target="tpu_custom_call" | custom-call | flops 536870912 | bytes 5242880 | tf_op jit(solution)/shard_map/pallas_call | solution.py:127
  92.0 4.2 %all-gather.2 = f32[256,512]{1,0:T(8,128)S(1)} all-gather(f32[128,512]{1,0:T(8,128)S(1)} %get-tuple-element.16), channel_id=4, replica_groups=mesh['zh'=2,'zl'=4,'yl'=2,'x'=4,'yh'=4,'c'=2] {'c'}, dimensions={0}, use_global_device_ids=true | all-gather | bytes 786432 | tf_op jit(solution)/shard_map/all_gather | solution.py:217
  96.2 0.1 shard_map.50
  96.3 11.8 %all_to_all.17.parts_ref = bf16[4,4,16,512]{3,2,1,0:T(8,128)(2,1)S(1)} all-to-all(bf16[4,4,16,512]{3,2,1,0:T(8,128)(2,1)S(1)} %bitcast.18), channel_id=1, replica_groups=mesh['zh'=2,'zl'=4,'yl'=2,'x'=4,'yh'=4,'c'=2] {'yh'}, dimensions={0} | all-to-all | bytes 524288 | tf_op jit(solution)/shard_map/all_to_all | solution.py:219
  108.1 0.7 shard_map.51
  (7 shorter events, 0.0 us)
Async XLA Ops:
  21.9 0.9 copy-start
  22.8 0.9 copy-start.1
  43.3 17.2 %collective-permute-start.2 = (bf16[32,4096]{1,0:T(8,128)(2,1)S(1)}, bf16[32,4096]{1,0:T(8,128)(2,1)S(1)}, u32[]{:S(2)}, u32[]{:S(2)}) collective-permute-start(bf16[32,4096]{1,0:T(8,128)(2,1)S(1)} %bitcast.21), channel_id=1, source_target_pairs={{0,72},{1,473},{2,74},{3,475},{4,76},{5,477},{6,78},{7,479},{8,64}... | collective-permute-start | bytes 786440 | tf_op jit(solution)/shard_map/ppermute | solution.py:50
  48.3 12.2 %collective-permute-start.1 = (bf16[32,4096]{1,0:T(8,128)(2,1)S(1)}, bf16[32,4096]{1,0:T(8,128)(2,1)S(1)}, u32[]{:S(2)}, u32[]{:S(2)}) collective-permute-start(bf16[32,4096]{1,0:T(8,128)(2,1)S(1)} %bitcast.22), channel_id=1, source_target_pairs={{0,64},{1,449},{2,66},{3,451},{4,68},{5,453},{6,70},{7,455},{8,72}... | collective-permute-start | bytes 786440 | tf_op jit(solution)/shard_map/ppermute | solution.py:50
  52.0 8.5 %collective-permute-start = (bf16[32,4096]{1,0:T(8,128)(2,1)S(1)}, bf16[32,4096]{1,0:T(8,128)(2,1)S(1)}, u32[]{:S(2)}, u32[]{:S(2)}) collective-permute-start(bf16[32,4096]{1,0:T(8,128)(2,1)S(1)} %bitcast.23), channel_id=1, source_target_pairs={{0,8},{1,25},{2,10},{3,27},{4,12},{5,29},{6,14},{7,31},{8,0},{9,17... | collective-permute-start | bytes 786440 | tf_op jit(solution)/shard_map/ppermute | solution.py:50
  60.7 12.0 %collective-permute-start.3 = (bf16[64,4096]{1,0:T(8,128)(2,1)S(1)}, bf16[64,4096]{1,0:T(8,128)(2,1)S(1)}, u32[]{:S(2)}, u32[]{:S(2)}) collective-permute-start(bf16[64,4096]{1,0:T(8,128)(2,1)S(1)} %get-tuple-element.18), channel_id=1, source_target_pairs={{0,24},{1,9},{2,26},{3,11},{4,28},{5,13},{6,30},{7,15},{8,16},{9,1... | collective-permute-start | bytes 1572872 | tf_op jit(solution)/shard_map/ppermute | solution.py:50
  62.6 13.4 %collective-permute-start.6 = (bf16[64,4096]{1,0:T(8,128)(2,1)S(1)}, bf16[64,4096]{1,0:T(8,128)(2,1)S(1)}, u32[]{:S(2)}, u32[]{:S(2)}) collective-permute-start(bf16[64,4096]{1,0:T(8,128)(2,1)S(1)} %get-tuple-element.17), channel_id=1, source_target_pairs={{0,448},{1,65},{2,450},{3,67},{4,452},{5,69},{6,454},{7,71},{8,456... | collective-permute-start | bytes 1572872 | tf_op jit(solution)/shard_map/ppermute | solution.py:50
  67.4 12.5 %collective-permute-start.5 = (bf16[64,4096]{1,0:T(8,128)(2,1)S(1)}, bf16[64,4096]{1,0:T(8,128)(2,1)S(1)}, u32[]{:S(2)}, u32[]{:S(2)}) collective-permute-start(bf16[64,4096]{1,0:T(8,128)(2,1)S(1)} %get-tuple-element.18), channel_id=1, source_target_pairs={{0,448},{1,65},{2,450},{3,67},{4,452},{5,69},{6,454},{7,71},{8,456... | collective-permute-start | bytes 1572872 | tf_op jit(solution)/shard_map/ppermute | solution.py:50
  69.3 12.1 %collective-permute-start.4 = (bf16[64,4096]{1,0:T(8,128)(2,1)S(1)}, bf16[64,4096]{1,0:T(8,128)(2,1)S(1)}, u32[]{:S(2)}, u32[]{:S(2)}) collective-permute-start(bf16[64,4096]{1,0:T(8,128)(2,1)S(1)} %get-tuple-element.17), channel_id=1, source_target_pairs={{0,24},{1,9},{2,26},{3,11},{4,28},{5,13},{6,30},{7,15},{8,16},{9,1... | collective-permute-start | bytes 1572872 | tf_op jit(solution)/shard_map/ppermute | solution.py:50
  72.7 17.7 %collective-permute-start.7 = (bf16[64,4096]{1,0:T(8,128)(2,1)S(1)}, bf16[64,4096]{1,0:T(8,128)(2,1)S(1)}, u32[]{:S(2)}, u32[]{:S(2)}) collective-permute-start(bf16[64,4096]{1,0:T(8,128)(2,1)S(1)} %collective-permute-done.3.pre_1a_ref), channel_id=1, source_target_pairs={{0,448},{1,65},{2,450},{3,67},{4,452},{5,69},{6,454},{7,71},{8,456... | collective-permute-start | bytes 1572872 | tf_op jit(solution)/shard_map/ppermute | solution.py:50
  76.1 14.3 %collective-permute-start.8 = (bf16[64,4096]{1,0:T(8,128)(2,1)S(1)}, bf16[64,4096]{1,0:T(8,128)(2,1)S(1)}, u32[]{:S(2)}, u32[]{:S(2)}) collective-permute-start(bf16[64,4096]{1,0:T(8,128)(2,1)S(1)} %collective-permute-done.6.pre_b_ref), channel_id=1, source_target_pairs={{0,24},{1,9},{2,26},{3,11},{4,28},{5,13},{6,30},{7,15},{8,16},{9,1... | collective-permute-start | bytes 1572872 | tf_op jit(solution)/shard_map/ppermute | solution.py:50

commit v3 on v2

v3 whole, which is shorter than its diff:
```python
import itertools

import jax
import jax.numpy as jnp
from jax import lax
from jax.experimental import pallas as pl
from jax.experimental.pallas import tpu as pltpu
from jax.sharding import Mesh
from jax.sharding import PartitionSpec as P

NAMES = ("zh", "zl", "yl", "x", "yh", "c")
SIZES = (2, 4, 2, 4, 4, 2)
WHOLE = pl.BlockSpec(memory_space=pltpu.VMEM)
BIG = pltpu.CompilerParams(vmem_limit_bytes=24 * 1024 * 1024)
SMALL = pltpu.CompilerParams(vmem_limit_bytes=12 * 1024 * 1024)


def near(axis, core):
    return (1, 3) if (axis == "x") == (core == 0) else (3, 1)


def device_index(zh, zl, yl, x, yh, c):
    index = 0
    for size, at in zip(SIZES, (zh, zl, yl, x, yh, c)):
        index = index * size + at
    return index


def z_neighbour(z, mask):
    return z ^ 1 if mask == 1 else (z + (1 if z % 2 else -1)) % 8


def every_device():
    return itertools.product(range(8), range(2), range(4), range(4), range(2))


def square_groups():
    groups = {}
    for z, yl, x, yh, c in every_device():
        x_pair, z_pair = (x, x ^ near("x", c)[0]), (z, z_neighbour(z, near("z", c)[0]))
        by_parity = lambda pair: sorted(pair, key=lambda at: at % 2)
        corners = [(z2, x2) for z2 in by_parity(z_pair) for x2 in by_parity(x_pair)]
        groups[tuple(device_index(z2 // 4, z2 % 4, yl, x2, yh, c) for z2, x2 in corners)] = None
    return [list(group) for group in groups]


def step_pairs(along_x):
    pairs = []
    for z, yl, x, yh, c in every_device():
        z2, x2 = (z, x ^ near("x", c)[1]) if along_x else (z_neighbour(z, near("z", c)[1]), x)
        pairs.append((device_index(z // 4, z % 4, yl, x, yh, c), device_index(z2 // 4, z2 % 4, yl, x2, yh, c)))
    return pairs


def exchange(block, along_x):
    return lax.ppermute(block, NAMES, step_pairs(along_x))


def three_parts(value):
    top = value.astype(jnp.bfloat16)
    rest = value - top.astype(jnp.float32)
    middle = rest.astype(jnp.bfloat16)
    low = (rest - middle.astype(jnp.float32)).astype(jnp.bfloat16)
    return jnp.concatenate([top, middle, low])


def prepare_kernel(query_ref, out_inv_ref, in_inv_ref, copies_ref, own_ref, factor_ref, rows, sems):
    feat = lax.axis_index("yh") * 2 + lax.axis_index("c")
    moves = [pltpu.make_async_copy(query_ref, copies_ref.at[copy], sems.at[copy]) for copy in range(4)]
    own_rows = out_inv_ref.at[:, pl.ds(pl.multiple_of(feat * 16, 16), 16), :]
    moves.append(pltpu.make_async_copy(own_rows, rows, sems.at[4]))
    moves.append(pltpu.make_async_copy(in_inv_ref, factor_ref, sems.at[5]))
    for move in moves:
        move.start()
    moves[4].wait()
    for layer in range(2):
        own_ref[layer] = three_parts(rows[layer])
    for move in moves[:4] + moves[5:]:
        move.wait()


def prepare(queries, out_inv, in_inv):
    far = pl.BlockSpec(memory_space=pltpu.HBM)
    return pl.pallas_call(
        prepare_kernel,
        out_shape=(
            jax.ShapeDtypeStruct((4,) + queries.shape, jnp.bfloat16),
            jax.ShapeDtypeStruct((2, 48, 128), jnp.bfloat16),
            jax.ShapeDtypeStruct((2, 128, 128), jnp.float32),
        ),
        in_specs=[far] * 3,
        out_specs=(WHOLE,) * 3,
        scratch_shapes=[pltpu.VMEM((2, 16, 128), jnp.float32), pltpu.SemaphoreType.DMA((6,))],
        cost_estimate=pl.CostEstimate(flops=10_000, bytes_accessed=700_000, transcendentals=0),
        compiler_params=SMALL,
    )(*(pltpu.with_memory_space_constraint(each, pltpu.HBM) for each in (queries, out_inv, in_inv)))


def precond_kernel(raw_ref, own_ref, in_inv_ref, pre_ref):
    for layer in range(2):
        mixed = []
        for q in range(8):
            whole = jnp.concatenate([raw_ref[f % 2, f // 2, q, layer] for f in range(8)])
            parts = jnp.dot(own_ref[layer], whole, preferred_element_type=jnp.float32)
            mixed.append((parts[32:] + parts[16:32]) + parts[:16])
        rows = jnp.dot(
            jnp.concatenate(mixed),
            in_inv_ref[layer],
            precision=lax.Precision.HIGHEST,
            preferred_element_type=jnp.float32,
        )
        pre_ref[:, layer] = rows.astype(jnp.bfloat16).reshape(8, 16, 128)


def precondition(raw, own, in_inv):
    return pl.pallas_call(
        precond_kernel,
        out_shape=jax.ShapeDtypeStruct((8, 2, 16, 128), jnp.bfloat16),
        in_specs=[WHOLE] * 3,
        out_specs=WHOLE,
        cost_estimate=pl.CostEstimate(flops=100_000_000, bytes_accessed=1_000_000, transcendentals=0),
        compiler_params=SMALL,
    )(raw, own, in_inv)


def flatten_kernel(train_ref, flat_ref, held, sems):
    parts = 4
    rows = held.shape[0] // parts
    moves = []
    for part in range(parts):
        window = pl.ds(part * rows, rows)
        moves.append(pltpu.make_async_copy(train_ref.at[window], held.at[window], sems.at[part]))
        moves[part].start()
    for part in range(parts):
        moves[part].wait()
        window = pl.ds(part * rows, rows)
        flat_ref[window, :] = held[window].reshape(rows, 4096)


def flatten(train):
    return pl.pallas_call(
        flatten_kernel,
        out_shape=jax.ShapeDtypeStruct((512, 4096), jnp.bfloat16),
        in_specs=[pl.BlockSpec(memory_space=pltpu.HBM)],
        out_specs=WHOLE,
        scratch_shapes=[pltpu.VMEM((512, 32, 128), jnp.bfloat16), pltpu.SemaphoreType.DMA((4,))],
        cost_estimate=pl.CostEstimate(flops=0, bytes_accessed=8_388_608, transcendentals=0),
        compiler_params=BIG,
    )(pltpu.with_memory_space_constraint(train, pltpu.HBM))


def nt_dot(a, b):
    return lax.dot_general(a, b, (((1,), (1,)), ((), ())), preferred_element_type=jnp.float32)


def split_rows(pieces, keep_ref, send_ref):
    core = lax.axis_index("c")
    for index, (piece, base) in enumerate(pieces):
        rows = slice(index * 64, index * 64 + 64)
        keep_ref[rows] = piece[pl.ds(pl.multiple_of(base + core * 64, 64), 64), :]
        send_ref[rows] = piece[pl.ds(pl.multiple_of(base + 64 - core * 64, 64), 64), :]


def score_kernel(*refs):
    *pieces, train_ref, keep_ref, send_ref, scores = refs
    scores[...] = nt_dot(jnp.concatenate([piece[...] for piece in pieces]), train_ref[...])
    split_rows(((scores, 0), (scores, 128)), keep_ref, send_ref)


def half_scores(pieces, train):
    half = jax.ShapeDtypeStruct((128, 512), jnp.float32)
    return pl.pallas_call(
        score_kernel,
        out_shape=(half, half),
        in_specs=[WHOLE] * (len(pieces) + 1),
        out_specs=(WHOLE, WHOLE),
        scratch_shapes=[pltpu.VMEM((256, 512), jnp.float32)],
        cost_estimate=pl.CostEstimate(flops=1_073_741_824, bytes_accessed=6_291_456, transcendentals=0),
        compiler_params=BIG,
    )(*pieces, train)


def block_places(half, core):
    x_first, x_second = [jnp.where(core == 0, near("x", 0)[step], near("x", 1)[step]) for step in range(2)]
    z_first, z_second = [jnp.where(core == 0, near("z", 0)[step], near("z", 1)[step]) for step in range(2)]
    x = lax.axis_index("x")
    z = lax.axis_index("zl") ^ (z_second if half else 0)
    z1 = jnp.where((z & 1) == lax.axis_index("c"), z, z ^ z_first) >> 1
    places = []
    for x_base in (x, x ^ x_second):
        for parity in range(2):
            x_of = jnp.where((x_base & 1) == parity, x_base, x_base ^ x_first)
            places += [(2 * zh + z1) * 4 + x_of for zh in range(2)]
    return places


def combine_kernel(keep_0_ref, keep_1_ref, got_0_ref, got_1_ref, out_ref, total):
    core = lax.axis_index("c")
    for half, keep_ref in enumerate((keep_0_ref, keep_1_ref)):
        for block, place in enumerate(block_places(half, core)):
            total[place] = keep_ref[block * 16 : block * 16 + 16]
    for half, got_ref in enumerate((got_0_ref, got_1_ref)):
        for block, place in enumerate(block_places(half, 1 - core)):
            total[place] = total[place] + got_ref[1 - core, block * 16 : block * 16 + 16]
    out_ref[...] = total[...].astype(jnp.bfloat16)


def combine(keeps, gots):
    return pl.pallas_call(
        combine_kernel,
        out_shape=jax.ShapeDtypeStruct((16, 16, 512), jnp.bfloat16),
        in_specs=[WHOLE] * 4,
        out_specs=WHOLE,
        scratch_shapes=[pltpu.VMEM((16, 16, 512), jnp.float32)],
        cost_estimate=pl.CostEstimate(flops=262_144, bytes_accessed=2_000_000, transcendentals=0),
        compiler_params=SMALL,
    )(*keeps, *gots)


def sum_kernel(parts_ref, out_ref):
    for x in range(4):
        total = parts_ref[0, x].astype(jnp.float32)
        for chip in range(1, 4):
            total = total + parts_ref[chip, x].astype(jnp.float32)
        out_ref[x * 8 : x * 8 + 8] = total[:8]
        out_ref[32 + x * 8 : 40 + x * 8] = total[8:]


def final_sum(parts):
    return pl.pallas_call(
        sum_kernel,
        out_shape=jax.ShapeDtypeStruct((64, 512), jnp.float32),
        in_specs=[WHOLE],
        out_specs=WHOLE,
        cost_estimate=pl.CostEstimate(flops=131_072, bytes_accessed=400_000, transcendentals=0),
        compiler_params=SMALL,
    )(parts)


def body(train_grads, query_grads, out_inv, in_inv):
    copies, own, factor = prepare(query_grads, out_inv, in_inv)
    raw = lax.all_gather(lax.all_to_all(copies, "yh", 0, 0, tiled=True), "c")
    pre = precondition(raw, own, factor).reshape(8, 32, 128)
    pre = lax.all_gather(lax.all_gather(pre, "zh"), "yl", axis=1)
    held = pre.reshape(32, 4096)
    train = flatten(train_grads.reshape(512, 32, 128))
    square = lax.all_to_all(
        jnp.broadcast_to(held[None], (4,) + held.shape), NAMES, 0, 0, tiled=True, axis_index_groups=square_groups()
    ).reshape(128, 4096)
    first, second = square[:64], square[64:]
    x_first, z_second = exchange(first, True), exchange(second, False)
    x_second, z_first = exchange(second, True), exchange(first, False)
    both_first, both_second = exchange(x_first, False), exchange(z_second, True)

    keep_0, send_0 = half_scores((square, x_first, x_second), train)
    got_0 = lax.all_gather(send_0, "c")
    keep_1, send_1 = half_scores((z_first, z_second, both_first, both_second), train)
    got_1 = lax.all_gather(send_1, "c")
    chip_sum = combine((keep_0, keep_1), (got_0, got_1))
    parts = lax.all_to_all(chip_sum.reshape(4, 4, 16, 512), "yh", 0, 0, tiled=True)
    return final_sum(parts).T


def solution(mesh):
    fine = Mesh(mesh.devices.reshape(SIZES), NAMES)
    rows, feat = ("zh", "zl", "yl", "x"), ("yh", "c")
    placed = (P(rows, None, feat, None), P(rows, None, feat, None), P(), P())
    return jax.shard_map(
        body, mesh=fine, in_specs=placed, out_specs=P(rows, feat), check_vma=False
    )
```

time: 110 us -> 104 us (0.945)
  blocking collectives: 63.5 us -> 73.2 us
  local copies, waits for them, and re-layouts: 9.23 us -> 0.29 us
  starting transfers between devices: 28 us -> 21.7 us
  Pallas kernels: 5.9 us -> 7.92 us
  waiting for transfers between devices: 1.87 us -> 0.02 us
    all_gather x0 -> x2, blocking collectives: none -> 16 us  [body(): pre = lax.all_gather(lax.all_gather(pre, 'zh'), 'yl', axis=1)]
    unnamed x5 -> x1, local copies, waits for them, and re-layouts: 8.16 us -> 0.11 us
    ppermute x9 -> x6, starting transfers between devices: 28 us -> 21.7 us  [exchange(): return lax.ppermute(block, NAMES, step_pairs(along_x))]
    all_to_all x1, blocking collectives: 18.8 us -> 14.8 us  [body(): lax.all_to_all(jnp.broadcast_to(held[None], (4,) + held.shape), NAMES, 0,...]
    all_gather x1, blocking collectives: 7.7 us -> 5.22 us  [body(): got_0 = lax.all_gather(send_0, 'c')]
    pallas_call x4 -> x5, Pallas kernels: 5.08 us -> 7.1 us  [the longest x2 2.67 us: half_scores(): pl.pallas_call(score_kernel, out_shape=(half, half), in_specs=[WHOLE] * (...]
    ppermute x9 -> x6, waiting for transfers between devices: 1.87 us -> 0.02 us  [exchange(): return lax.ppermute(block, NAMES, step_pairs(along_x))]
  transfers between devices with their start and end apart: 9 -> 6, of which waited for: 1 -> 0; matrix products, arithmetic and copies ran while one was open for 6% -> 0% of each run, Pallas kernels for 3% -> 4%
where the time goes in v3:
time: 104 us; the launch traced here: 103 us
  blocking collectives  73.2 us (70%)
  starting transfers between devices  21.7 us (21%)
  Pallas kernels  7.92 us (8%)
    ppermute x6, starting transfers between devices, exchange(): return lax.ppermute(block, NAMES, step_pairs(along_x))  21.7 us
    all_to_all x1, blocking collectives, body(): raw = lax.all_gather(lax.all_to_all(copies, 'yh', 0, 0, tiled=True), 'c')  16.4 us
    all_gather x2, blocking collectives, body(): pre = lax.all_gather(lax.all_gather(pre, 'zh'), 'yl', axis=1)  16 us
    all_to_all x1, blocking collectives, body(): lax.all_to_all(jnp.broadcast_to(held[None], (4,) + held.shape), NAMES, 0,...  14.8 us
    all_to_all x1, blocking collectives, body(): lax.all_to_all(chip_sum.reshape(4, 4, 16, 512), 'yh', 0, 0, tiled=True)  11.8 us
    all_gather x1, blocking collectives, body(): got_0 = lax.all_gather(send_0, 'c')  5.22 us
    all_gather x1, blocking collectives, body(): raw = lax.all_gather(lax.all_to_all(copies, 'yh', 0, 0, tiled=True), 'c')  4.59 us
    all_gather x1, blocking collectives, body(): got_1 = lax.all_gather(send_1, 'c')  4.46 us
  transfers between devices with their start and end apart: 6, of which 0 were waited for; matrix products, arithmetic and copies ran while one was open for 0% of the time, Pallas kernels for 4%

profile of v3, /device:TPU:1, one launch (start us, length us, event | category | flops | bytes accessed | tf_op | source)
XLA Modules:
  0.0 103.4 jit_solution(3034022558909171516)
XLA Ops:
  0.0 1.1 %shard_map.46 = (bf16[4,8,2,16,128]{4,3,2,1,0:T(8,128)(2,1)S(1)}, bf16[2,48,128]{2,1,0:T(8,128)(2,1)S(1)}, f32[2,128,128]{2,1,0:T(8,128)S(1)}) custom-call(bf16[8,2,16,128]{3,2,1,0:T(8,128)(2,1)} %query_ref.1, f32[2,128,128]{2,1,0:T(8,128)} %out_inv_ref.1, f32[2,128,128]{2,1,0:T(8,128)} %in_inv_ref.1), custom_call_target="tpu_custom_call" | custom-call | flops 10000 | bytes 700000 | tf_op jit(solution)/shard_map/pallas_call | solution.py:84
  1.1 16.4 %all_to_all.15 = bf16[4,8,2,16,128]{4,3,2,1,0:T(8,128)(2,1)S(1)} all-to-all(bf16[4,8,2,16,128]{4,3,2,1,0:T(8,128)(2,1)S(1)} %get-tuple-element.12), channel_id=1, replica_groups=mesh['zh'=2,'zl'=4,'yl'=2,'x'=4,'yh'=4,'c'=2] {'yh'}, dimensions={0} | all-to-all | bytes 524288 | tf_op jit(solution)/shard_map/all_to_all | solution.py:242
  17.6 4.6 %all-gather = bf16[8,8,2,16,128]{4,3,2,1,0:T(8,128)(2,1)S(1)} all-gather(bf16[4,8,2,16,128]{4,3,2,1,0:T(8,128)(2,1)S(1)} %all_to_all.15), channel_id=2, replica_groups=mesh['zh'=2,'zl'=4,'yl'=2,'x'=4,'yh'=4,'c'=2] {'c'}, dimensions={0}, use_global_device_ids=true | all-gather | bytes 786432 | tf_op jit(solution)/shard_map/all_gather | solution.py:242
  22.1 0.7 shard_map.47
  22.8 11.5 %all_gather.29 = bf16[2,8,32,128]{3,2,1,0:T(8,128)(2,1)S(1)} all-gather(bf16[1,8,32,128]{3,2,1,0:T(8,128)(2,1)S(1)} %bitcast.20), channel_id=1, replica_groups=mesh['zh'=2,'zl'=4,'yl'=2,'x'=4,'yh'=4,'c'=2] {'zh'}, dimensions={0}, use_global_device_ids=true | all-gather | bytes 196608 | tf_op jit(solution)/shard_map/all_gather | solution.py:244
  34.4 4.5 %all-gather.1 = bf16[2,16,32,128]{3,2,1,0:T(8,128)(2,1)S(1)} all-gather(bf16[2,8,32,128]{3,2,1,0:T(8,128)(2,1)S(1)} %all_gather.29), channel_id=3, replica_groups=mesh['zh'=2,'zl'=4,'yl'=2,'x'=4,'yh'=4,'c'=2] {'yl'}, dimensions={1}, use_global_device_ids=true | all-gather | bytes 393216 | tf_op jit(solution)/shard_map/all_gather | solution.py:244
  38.9 0.1 copy.7
  39.0 0.1 broadcast_in_dim.8
  39.1 14.8 %all_to_all.16 = bf16[4,32,4096]{2,1,0:T(8,128)(2,1)S(1)} all-to-all(bf16[4,32,4096]{2,1,0:T(8,128)(2,1)S(1)} %broadcast_in_dim.8), channel_id=1, replica_groups={{0,8,448,456},{1,25,65,89},{2,10,450,458},{3,27,67,91},{4,12,452,460},{..., dimensions={0} | all-to-all | bytes 2097152 | tf_op jit(solution)/shard_map/all_to_all | solution.py:247
  53.8 0.1 fusion
  53.9 1.9 %collective-permute-start = (bf16[64,4096]{1,0:T(8,128)(2,1)S(1)}, bf16[64,4096]{1,0:T(8,128)(2,1)S(1)}, u32[]{:S(2)}, u32[]{:S(2)}) collective-permute-start(bf16[64,4096]{1,0:T(8,128)(2,1)S(1)} %bitcast.24), channel_id=1, source_target_pairs={{0,24},{1,9},{2,26},{3,11},{4,28},{5,13},{6,30},{7,15},{8,16},{9,1... | collective-permute-start | bytes 1572872 | tf_op jit(solution)/shard_map/ppermute | solution.py:56
  55.9 8.1 %collective-permute-start.3 = (bf16[64,4096]{1,0:T(8,128)(2,1)S(1)}, bf16[64,4096]{1,0:T(8,128)(2,1)S(1)}, u32[]{:S(2)}, u32[]{:S(2)}) collective-permute-start(bf16[64,4096]{1,0:T(8,128)(2,1)S(1)} %bitcast.26), channel_id=1, source_target_pairs={{0,64},{1,449},{2,66},{3,451},{4,68},{5,453},{6,70},{7,455},{8,72}... | collective-permute-start | bytes 1572872 | tf_op jit(solution)/shard_map/ppermute | solution.py:56
  63.9 3.4 %collective-permute-start.1 = (bf16[64,4096]{1,0:T(8,128)(2,1)S(1)}, bf16[64,4096]{1,0:T(8,128)(2,1)S(1)}, u32[]{:S(2)}, u32[]{:S(2)}) collective-permute-start(bf16[64,4096]{1,0:T(8,128)(2,1)S(1)} %bitcast.27), channel_id=1, source_target_pairs={{0,24},{1,9},{2,26},{3,11},{4,28},{5,13},{6,30},{7,15},{8,16},{9,1... | collective-permute-start | bytes 1572872 | tf_op jit(solution)/shard_map/ppermute | solution.py:56
  67.3 1.9 %collective-permute-start.2 = (bf16[64,4096]{1,0:T(8,128)(2,1)S(1)}, bf16[64,4096]{1,0:T(8,128)(2,1)S(1)}, u32[]{:S(2)}, u32[]{:S(2)}) collective-permute-start(bf16[64,4096]{1,0:T(8,128)(2,1)S(1)} %bitcast.25), channel_id=1, source_target_pairs={{0,64},{1,449},{2,66},{3,451},{4,68},{5,453},{6,70},{7,455},{8,72}... | collective-permute-start | bytes 1572872 | tf_op jit(solution)/shard_map/ppermute | solution.py:56
  69.2 0.0 collective-permute-done.refs_1_
  69.2 4.6 %collective-permute-start.4 = (bf16[64,4096]{1,0:T(8,128)(2,1)S(1)}, bf16[64,4096]{1,0:T(8,128)(2,1)S(1)}, u32[]{:S(2)}, u32[]{:S(2)}) collective-permute-start(bf16[64,4096]{1,0:T(8,128)(2,1)S(1)} %collective-permute-done.refs_1_), channel_id=1, source_target_pairs={{0,64},{1,449},{2,66},{3,451},{4,68},{5,453},{6,70},{7,455},{8,72}... | collective-permute-start | bytes 1572872 | tf_op jit(solution)/shard_map/ppermute | solution.py:56
  73.8 0.0 collective-permute-done.3.refs_1_
  73.8 1.9 %collective-permute-start.5 = (bf16[64,4096]{1,0:T(8,128)(2,1)S(1)}, bf16[64,4096]{1,0:T(8,128)(2,1)S(1)}, u32[]{:S(2)}, u32[]{:S(2)}) collective-permute-start(bf16[64,4096]{1,0:T(8,128)(2,1)S(1)} %collective-permute-done.3.refs_1_), channel_id=1, source_target_pairs={{0,24},{1,9},{2,26},{3,11},{4,28},{5,13},{6,30},{7,15},{8,16},{9,1... | collective-permute-start | bytes 1572872 | tf_op jit(solution)/shard_map/ppermute | solution.py:56
  75.7 2.6 %shard_map.48.refs_3_.refs_4_ = bf16[512,4096]{1,0:T(8,128)(2,1)S(1)} custom-call(bf16[512,32,128]{2,1,0:T(8,128)(2,1)} %bitcast.21), custom_call_target="tpu_custom_call" | custom-call | bytes 8388608 | tf_op jit(solution)/shard_map/pallas_call | solution.py:141
  78.4 0.0 collective-permute-done.1.refs_2_
  78.4 1.3 %shard_map.49 = (f32[128,512]{1,0:T(8,128)S(1)}, f32[128,512]{1,0:T(8,128)S(1)}) custom-call(bf16[128,4096]{1,0:T(8,128)(2,1)S(1)} %bitcast.15, bf16[64,4096]{1,0:T(8,128)(2,1)S(1)} %collective-permute-done.refs_1_, bf16[64,4096]{1,0:T(8,128)(2,1)S(1)} %collective-permute-done.1.refs_2_, bf16[512,4096]{1,0:T(8,128)(2,1)S(1)} %shard_map.48.refs_3_.refs_4_), custom_call_target="tpu_custom_call" | custom-call | flops 1073741824 | bytes 6291456 | tf_op jit(solution)/shard_map/pallas_call | solution.py:172
  79.7 5.2 %all-gather.2 = f32[256,512]{1,0:T(8,128)S(1)} all-gather(f32[128,512]{1,0:T(8,128)S(1)} %get-tuple-element.17), channel_id=4, replica_groups=mesh['zh'=2,'zl'=4,'yl'=2,'x'=4,'yh'=4,'c'=2] {'c'}, dimensions={0}, use_global_device_ids=true | all-gather | bytes 786432 | tf_op jit(solution)/shard_map/all_gather | solution.py:256
  85.0 0.0 collective-permute-done.2.refs_0_
  85.0 0.0 collective-permute-done.4.refs_2_
  85.0 0.0 collective-permute-done.5.refs_3_
  85.0 1.3 %shard_map.50 = (f32[128,512]{1,0:T(8,128)S(1)}, f32[128,512]{1,0:T(8,128)S(1)}) custom-call(bf16[64,4096]{1,0:T(8,128)(2,1)S(1)} %collective-permute-done.2.refs_0_, bf16[64,4096]{1,0:T(8,128)(2,1)S(1)} %collective-permute-done.3.refs_1_, bf16[64,4096]{1,0:T(8,128)(2,1)S(1)} %collective-permute-done.4.refs_2_, ...), custom_call_target="tpu_custom_call" | custom-call | flops 1073741824 | bytes 6291456 | tf_op jit(solution)/shard_map/pallas_call | solution.py:172
  86.3 4.5 %all-gather.3 = f32[256,512]{1,0:T(8,128)S(1)} all-gather(f32[128,512]{1,0:T(8,128)S(1)} %get-tuple-element.18), channel_id=5, replica_groups=mesh['zh'=2,'zl'=4,'yl'=2,'x'=4,'yh'=4,'c'=2] {'c'}, dimensions={0}, use_global_device_ids=true | all-gather | bytes 786432 | tf_op jit(solution)/shard_map/all_gather | solution.py:258
  90.8 0.1 shard_map.51
  90.9 11.8 %all_to_all.17.parts_ref = bf16[4,4,16,512]{3,2,1,0:T(8,128)(2,1)S(1)} all-to-all(bf16[4,4,16,512]{3,2,1,0:T(8,128)(2,1)S(1)} %bitcast.19), channel_id=1, replica_groups=mesh['zh'=2,'zl'=4,'yl'=2,'x'=4,'yh'=4,'c'=2] {'yh'}, dimensions={0} | all-to-all | bytes 524288 | tf_op jit(solution)/shard_map/all_to_all | solution.py:260
  102.7 0.7 shard_map.52
Async XLA Ops:
  53.9 15.3 %collective-permute-start = (bf16[64,4096]{1,0:T(8,128)(2,1)S(1)}, bf16[64,4096]{1,0:T(8,128)(2,1)S(1)}, u32[]{:S(2)}, u32[]{:S(2)}) collective-permute-start(bf16[64,4096]{1,0:T(8,128)(2,1)S(1)} %bitcast.24), channel_id=1, source_target_pairs={{0,24},{1,9},{2,26},{3,11},{4,28},{5,13},{6,30},{7,15},{8,16},{9,1... | collective-permute-start | bytes 1572872 | tf_op jit(solution)/shard_map/ppermute | solution.py:56
  55.9 18.0 %collective-permute-start.3 = (bf16[64,4096]{1,0:T(8,128)(2,1)S(1)}, bf16[64,4096]{1,0:T(8,128)(2,1)S(1)}, u32[]{:S(2)}, u32[]{:S(2)}) collective-permute-start(bf16[64,4096]{1,0:T(8,128)(2,1)S(1)} %bitcast.26), channel_id=1, source_target_pairs={{0,64},{1,449},{2,66},{3,451},{4,68},{5,453},{6,70},{7,455},{8,72}... | collective-permute-start | bytes 1572872 | tf_op jit(solution)/shard_map/ppermute | solution.py:56
  63.9 14.5 %collective-permute-start.1 = (bf16[64,4096]{1,0:T(8,128)(2,1)S(1)}, bf16[64,4096]{1,0:T(8,128)(2,1)S(1)}, u32[]{:S(2)}, u32[]{:S(2)}) collective-permute-start(bf16[64,4096]{1,0:T(8,128)(2,1)S(1)} %bitcast.27), channel_id=1, source_target_pairs={{0,24},{1,9},{2,26},{3,11},{4,28},{5,13},{6,30},{7,15},{8,16},{9,1... | collective-permute-start | bytes 1572872 | tf_op jit(solution)/shard_map/ppermute | solution.py:56
  67.3 17.7 %collective-permute-start.2 = (bf16[64,4096]{1,0:T(8,128)(2,1)S(1)}, bf16[64,4096]{1,0:T(8,128)(2,1)S(1)}, u32[]{:S(2)}, u32[]{:S(2)}) collective-permute-start(bf16[64,4096]{1,0:T(8,128)(2,1)S(1)} %bitcast.25), channel_id=1, source_target_pairs={{0,64},{1,449},{2,66},{3,451},{4,68},{5,453},{6,70},{7,455},{8,72}... | collective-permute-start | bytes 1572872 | tf_op jit(solution)/shard_map/ppermute | solution.py:56
  69.2 15.7 %collective-permute-start.4 = (bf16[64,4096]{1,0:T(8,128)(2,1)S(1)}, bf16[64,4096]{1,0:T(8,128)(2,1)S(1)}, u32[]{:S(2)}, u32[]{:S(2)}) collective-permute-start(bf16[64,4096]{1,0:T(8,128)(2,1)S(1)} %collective-permute-done.refs_1_), channel_id=1, source_target_pairs={{0,64},{1,449},{2,66},{3,451},{4,68},{5,453},{6,70},{7,455},{8,72}... | collective-permute-start | bytes 1572872 | tf_op jit(solution)/shard_map/ppermute | solution.py:56
  73.8 11.2 %collective-permute-start.5 = (bf16[64,4096]{1,0:T(8,128)(2,1)S(1)}, bf16[64,4096]{1,0:T(8,128)(2,1)S(1)}, u32[]{:S(2)}, u32[]{:S(2)}) collective-permute-start(bf16[64,4096]{1,0:T(8,128)(2,1)S(1)} %collective-permute-done.3.refs_1_), channel_id=1, source_target_pairs={{0,24},{1,9},{2,26},{3,11},{4,28},{5,13},{6,30},{7,15},{8,16},{9,1... | collective-permute-start | bytes 1572872 | tf_op jit(solution)/shard_map/ppermute | solution.py:56

commit v4 on v3

--- a/solution.py
+++ b/solution.py
@@ -64,18 +64,15 @@
     return jnp.concatenate([top, middle, low])
 
 
-def prepare_kernel(query_ref, out_inv_ref, in_inv_ref, copies_ref, own_ref, factor_ref, rows, sems):
+def prepare_kernel(query_ref, out_inv_ref, in_inv_ref, copies_ref, own_ref, factor_ref, sems):
     feat = lax.axis_index("yh") * 2 + lax.axis_index("c")
     moves = [pltpu.make_async_copy(query_ref, copies_ref.at[copy], sems.at[copy]) for copy in range(4)]
     own_rows = out_inv_ref.at[:, pl.ds(pl.multiple_of(feat * 16, 16), 16), :]
-    moves.append(pltpu.make_async_copy(own_rows, rows, sems.at[4]))
+    moves.append(pltpu.make_async_copy(own_rows, own_ref, sems.at[4]))
     moves.append(pltpu.make_async_copy(in_inv_ref, factor_ref, sems.at[5]))
     for move in moves:
         move.start()
-    moves[4].wait()
-    for layer in range(2):
-        own_ref[layer] = three_parts(rows[layer])
-    for move in moves[:4] + moves[5:]:
+    for move in moves:
         move.wait()
 
 
@@ -85,23 +82,24 @@
         prepare_kernel,
         out_shape=(
             jax.ShapeDtypeStruct((4,) + queries.shape, jnp.bfloat16),
-            jax.ShapeDtypeStruct((2, 48, 128), jnp.bfloat16),
+            jax.ShapeDtypeStruct((2, 16, 128), jnp.float32),
             jax.ShapeDtypeStruct((2, 128, 128), jnp.float32),
         ),
         in_specs=[far] * 3,
         out_specs=(WHOLE,) * 3,
-        scratch_shapes=[pltpu.VMEM((2, 16, 128), jnp.float32), pltpu.SemaphoreType.DMA((6,))],
-        cost_estimate=pl.CostEstimate(flops=10_000, bytes_accessed=700_000, transcendentals=0),
+        scratch_shapes=[pltpu.SemaphoreType.DMA((6,))],
+        cost_estimate=pl.CostEstimate(flops=0, bytes_accessed=700_000, transcendentals=0),
         compiler_params=SMALL,
     )(*(pltpu.with_memory_space_constraint(each, pltpu.HBM) for each in (queries, out_inv, in_inv)))
 
 
 def precond_kernel(raw_ref, own_ref, in_inv_ref, pre_ref):
     for layer in range(2):
+        own = three_parts(own_ref[layer])
         mixed = []
         for q in range(8):
             whole = jnp.concatenate([raw_ref[f % 2, f // 2, q, layer] for f in range(8)])
-            parts = jnp.dot(own_ref[layer], whole, preferred_element_type=jnp.float32)
+            parts = jnp.dot(own, whole, preferred_element_type=jnp.float32)
             mixed.append((parts[32:] + parts[16:32]) + parts[:16])
         rows = jnp.dot(
             jnp.concatenate(mixed),
@@ -124,7 +122,7 @@
 
 
 def flatten_kernel(train_ref, flat_ref, held, sems):
-    parts = 4
+    parts = 8
     rows = held.shape[0] // parts
     moves = []
     for part in range(parts):
@@ -143,7 +141,7 @@
         out_shape=jax.ShapeDtypeStruct((512, 4096), jnp.bfloat16),
         in_specs=[pl.BlockSpec(memory_space=pltpu.HBM)],
         out_specs=WHOLE,
-        scratch_shapes=[pltpu.VMEM((512, 32, 128), jnp.bfloat16), pltpu.SemaphoreType.DMA((4,))],
+        scratch_shapes=[pltpu.VMEM((512, 32, 128), jnp.bfloat16), pltpu.SemaphoreType.DMA((8,))],
         cost_estimate=pl.CostEstimate(flops=0, bytes_accessed=8_388_608, transcendentals=0),
         compiler_params=BIG,
     )(pltpu.with_memory_space_constraint(train, pltpu.HBM))
@@ -194,7 +192,7 @@
     return places
 
 
-def combine_kernel(keep_0_ref, keep_1_ref, got_0_ref, got_1_ref, out_ref, total):
+def combine_kernel(keep_0_ref, keep_1_ref, got_0_ref, got_1_ref, out_ref, own_ref, total):
     core = lax.axis_index("c")
     for half, keep_ref in enumerate((keep_0_ref, keep_1_ref)):
         for block, place in enumerate(block_places(half, core)):
@@ -203,38 +201,43 @@
         for block, place in enumerate(block_places(half, 1 - core)):
             total[place] = total[place] + got_ref[1 - core, block * 16 : block * 16 + 16]
     out_ref[...] = total[...].astype(jnp.bfloat16)
+    own_ref[...] = total[pl.ds(lax.axis_index("yh") * 4, 4)]
 
 
 def combine(keeps, gots):
     return pl.pallas_call(
         combine_kernel,
-        out_shape=jax.ShapeDtypeStruct((16, 16, 512), jnp.bfloat16),
+        out_shape=(
+            jax.ShapeDtypeStruct((16, 16, 512), jnp.bfloat16),
+            jax.ShapeDtypeStruct((4, 16, 512), jnp.float32),
+        ),
         in_specs=[WHOLE] * 4,
-        out_specs=WHOLE,
+        out_specs=(WHOLE, WHOLE),
         scratch_shapes=[pltpu.VMEM((16, 16, 512), jnp.float32)],
         cost_estimate=pl.CostEstimate(flops=262_144, bytes_accessed=2_000_000, transcendentals=0),
         compiler_params=SMALL,
     )(*keeps, *gots)
 
 
-def sum_kernel(parts_ref, out_ref):
+def sum_kernel(parts_ref, own_ref, out_ref):
+    chip = lax.axis_index("yh")
     for x in range(4):
-        total = parts_ref[0, x].astype(jnp.float32)
-        for chip in range(1, 4):
-            total = total + parts_ref[chip, x].astype(jnp.float32)
+        total = own_ref[x]
+        for step in range(1, 4):
+            total = total + parts_ref[(chip + step) & 3, x].astype(jnp.float32)
         out_ref[x * 8 : x * 8 + 8] = total[:8]
         out_ref[32 + x * 8 : 40 + x * 8] = total[8:]
 
 
-def final_sum(parts):
+def final_sum(parts, own):
     return pl.pallas_call(
         sum_kernel,
         out_shape=jax.ShapeDtypeStruct((64, 512), jnp.float32),
-        in_specs=[WHOLE],
+        in_specs=[WHOLE] * 2,
         out_specs=WHOLE,
-        cost_estimate=pl.CostEstimate(flops=131_072, bytes_accessed=400_000, transcendentals=0),
-        compiler_params=SMALL,
-    )(parts)
+        cost_estimate=pl.CostEstimate(flops=131_072, bytes_accessed=500_000, transcendentals=0),
+        compiler_params=SMALL,
+    )(parts, own)
 
 
 def body(train_grads, query_grads, out_inv, in_inv):
@@ -256,9 +259,9 @@
     got_0 = lax.all_gather(send_0, "c")
     keep_1, send_1 = half_scores((z_first, z_second, both_first, both_second), train)
     got_1 = lax.all_gather(send_1, "c")
-    chip_sum = combine((keep_0, keep_1), (got_0, got_1))
+    chip_sum, own_sum = combine((keep_0, keep_1), (got_0, got_1))
     parts = lax.all_to_all(chip_sum.reshape(4, 4, 16, 512), "yh", 0, 0, tiled=True)
-    return final_sum(parts).T
+    return final_sum(parts, own_sum).T
 
 
 def solution(mesh):

time: 104 us -> 104 us (level)
  no operation moved by 1% of the time
where the time goes in v4:
time: 104 us; the launch traced here: 103 us
  blocking collectives  73.4 us (71%)
  starting transfers between devices  21.8 us (21%)
  Pallas kernels  7.81 us (8%)
    ppermute x6, starting transfers between devices, exchange(): return lax.ppermute(block, NAMES, step_pairs(along_x))  21.8 us
    all_to_all x1, blocking collectives, body(): raw = lax.all_gather(lax.all_to_all(copies, 'yh', 0, 0, tiled=True), 'c')  16.4 us
    all_gather x2, blocking collectives, body(): pre = lax.all_gather(lax.all_gather(pre, 'zh'), 'yl', axis=1)  16 us
    all_to_all x1, blocking collectives, body(): lax.all_to_all(jnp.broadcast_to(held[None], (4,) + held.shape), NAMES, 0,...  14.8 us
    all_to_all x1, blocking collectives, body(): lax.all_to_all(chip_sum.reshape(4, 4, 16, 512), 'yh', 0, 0, tiled=True)  11.8 us
    all_gather x1, blocking collectives, body(): got_0 = lax.all_gather(send_0, 'c')  5.22 us
    all_gather x1, blocking collectives, body(): raw = lax.all_gather(lax.all_to_all(copies, 'yh', 0, 0, tiled=True), 'c')  4.59 us
    all_gather x1, blocking collectives, body(): got_1 = lax.all_gather(send_1, 'c')  4.58 us
  transfers between devices with their start and end apart: 6, of which 0 were waited for; matrix products, arithmetic and copies ran while one was open for 0% of the time, Pallas kernels for 4%

profile of v4, /device:TPU:1, one launch (start us, length us, event | category | flops | bytes accessed | tf_op | source)
XLA Modules:
  0.0 103.4 jit_solution(11168486891988886629)
XLA Ops:
  0.0 1.1 %shard_map.46 = (bf16[4,8,2,16,128]{4,3,2,1,0:T(8,128)(2,1)S(1)}, f32[2,16,128]{2,1,0:T(8,128)S(1)}, f32[2,128,128]{2,1,0:T(8,128)S(1)}) custom-call(bf16[8,2,16,128]{3,2,1,0:T(8,128)(2,1)} %query_ref.1, f32[2,128,128]{2,1,0:T(8,128)} %out_inv_ref.1, f32[2,128,128]{2,1,0:T(8,128)} %in_inv_ref.1), custom_call_target="tpu_custom_call" | custom-call | bytes 700000 | tf_op jit(solution)/shard_map/pallas_call | solution.py:81
  1.1 16.4 %all_to_all.15 = bf16[4,8,2,16,128]{4,3,2,1,0:T(8,128)(2,1)S(1)} all-to-all(bf16[4,8,2,16,128]{4,3,2,1,0:T(8,128)(2,1)S(1)} %get-tuple-element.14), channel_id=1, replica_groups=mesh['zh'=2,'zl'=4,'yl'=2,'x'=4,'yh'=4,'c'=2] {'yh'}, dimensions={0} | all-to-all | bytes 524288 | tf_op jit(solution)/shard_map/all_to_all | solution.py:245
  17.6 4.6 %all-gather = bf16[8,8,2,16,128]{4,3,2,1,0:T(8,128)(2,1)S(1)} all-gather(bf16[4,8,2,16,128]{4,3,2,1,0:T(8,128)(2,1)S(1)} %all_to_all.15), channel_id=2, replica_groups=mesh['zh'=2,'zl'=4,'yl'=2,'x'=4,'yh'=4,'c'=2] {'c'}, dimensions={0}, use_global_device_ids=true | all-gather | bytes 786432 | tf_op jit(solution)/shard_map/all_gather | solution.py:245
  22.1 0.7 shard_map.47
  22.8 11.5 %all_gather.29 = bf16[2,8,32,128]{3,2,1,0:T(8,128)(2,1)S(1)} all-gather(bf16[1,8,32,128]{3,2,1,0:T(8,128)(2,1)S(1)} %bitcast.19), channel_id=1, replica_groups=mesh['zh'=2,'zl'=4,'yl'=2,'x'=4,'yh'=4,'c'=2] {'zh'}, dimensions={0}, use_global_device_ids=true | all-gather | bytes 196608 | tf_op jit(solution)/shard_map/all_gather | solution.py:247
  34.4 4.5 %all-gather.1 = bf16[2,16,32,128]{3,2,1,0:T(8,128)(2,1)S(1)} all-gather(bf16[2,8,32,128]{3,2,1,0:T(8,128)(2,1)S(1)} %all_gather.29), channel_id=3, replica_groups=mesh['zh'=2,'zl'=4,'yl'=2,'x'=4,'yh'=4,'c'=2] {'yl'}, dimensions={1}, use_global_device_ids=true | all-gather | bytes 393216 | tf_op jit(solution)/shard_map/all_gather | solution.py:247
  38.9 0.1 copy.7
  39.0 0.1 broadcast_in_dim.8
  39.1 14.8 %all_to_all.16 = bf16[4,32,4096]{2,1,0:T(8,128)(2,1)S(1)} all-to-all(bf16[4,32,4096]{2,1,0:T(8,128)(2,1)S(1)} %broadcast_in_dim.8), channel_id=1, replica_groups={{0,8,448,456},{1,25,65,89},{2,10,450,458},{3,27,67,91},{4,12,452,460},{..., dimensions={0} | all-to-all | bytes 2097152 | tf_op jit(solution)/shard_map/all_to_all | solution.py:250
  53.8 0.1 fusion
  53.9 1.9 %collective-permute-start = (bf16[64,4096]{1,0:T(8,128)(2,1)S(1)}, bf16[64,4096]{1,0:T(8,128)(2,1)S(1)}, u32[]{:S(2)}, u32[]{:S(2)}) collective-permute-start(bf16[64,4096]{1,0:T(8,128)(2,1)S(1)} %bitcast.24), channel_id=1, source_target_pairs={{0,24},{1,9},{2,26},{3,11},{4,28},{5,13},{6,30},{7,15},{8,16},{9,1... | collective-permute-start | bytes 1572872 | tf_op jit(solution)/shard_map/ppermute | solution.py:56
  55.9 8.1 %collective-permute-start.3 = (bf16[64,4096]{1,0:T(8,128)(2,1)S(1)}, bf16[64,4096]{1,0:T(8,128)(2,1)S(1)}, u32[]{:S(2)}, u32[]{:S(2)}) collective-permute-start(bf16[64,4096]{1,0:T(8,128)(2,1)S(1)} %bitcast.26), channel_id=1, source_target_pairs={{0,64},{1,449},{2,66},{3,451},{4,68},{5,453},{6,70},{7,455},{8,72}... | collective-permute-start | bytes 1572872 | tf_op jit(solution)/shard_map/ppermute | solution.py:56
  63.9 3.4 %collective-permute-start.1 = (bf16[64,4096]{1,0:T(8,128)(2,1)S(1)}, bf16[64,4096]{1,0:T(8,128)(2,1)S(1)}, u32[]{:S(2)}, u32[]{:S(2)}) collective-permute-start(bf16[64,4096]{1,0:T(8,128)(2,1)S(1)} %bitcast.27), channel_id=1, source_target_pairs={{0,24},{1,9},{2,26},{3,11},{4,28},{5,13},{6,30},{7,15},{8,16},{9,1... | collective-permute-start | bytes 1572872 | tf_op jit(solution)/shard_map/ppermute | solution.py:56
  67.3 1.9 %collective-permute-start.2 = (bf16[64,4096]{1,0:T(8,128)(2,1)S(1)}, bf16[64,4096]{1,0:T(8,128)(2,1)S(1)}, u32[]{:S(2)}, u32[]{:S(2)}) collective-permute-start(bf16[64,4096]{1,0:T(8,128)(2,1)S(1)} %bitcast.25), channel_id=1, source_target_pairs={{0,64},{1,449},{2,66},{3,451},{4,68},{5,453},{6,70},{7,455},{8,72}... | collective-permute-start | bytes 1572872 | tf_op jit(solution)/shard_map/ppermute | solution.py:56
  69.2 0.0 collective-permute-done.refs_1_
  69.2 4.6 %collective-permute-start.4 = (bf16[64,4096]{1,0:T(8,128)(2,1)S(1)}, bf16[64,4096]{1,0:T(8,128)(2,1)S(1)}, u32[]{:S(2)}, u32[]{:S(2)}) collective-permute-start(bf16[64,4096]{1,0:T(8,128)(2,1)S(1)} %collective-permute-done.refs_1_), channel_id=1, source_target_pairs={{0,64},{1,449},{2,66},{3,451},{4,68},{5,453},{6,70},{7,455},{8,72}... | collective-permute-start | bytes 1572872 | tf_op jit(solution)/shard_map/ppermute | solution.py:56
  73.8 0.0 collective-permute-done.3.refs_1_
  73.8 1.9 %collective-permute-start.5 = (bf16[64,4096]{1,0:T(8,128)(2,1)S(1)}, bf16[64,4096]{1,0:T(8,128)(2,1)S(1)}, u32[]{:S(2)}, u32[]{:S(2)}) collective-permute-start(bf16[64,4096]{1,0:T(8,128)(2,1)S(1)} %collective-permute-done.3.refs_1_), channel_id=1, source_target_pairs={{0,24},{1,9},{2,26},{3,11},{4,28},{5,13},{6,30},{7,15},{8,16},{9,1... | collective-permute-start | bytes 1572872 | tf_op jit(solution)/shard_map/ppermute | solution.py:56
  75.7 2.5 %shard_map.48.refs_3_.refs_4_ = bf16[512,4096]{1,0:T(8,128)(2,1)S(1)} custom-call(bf16[512,32,128]{2,1,0:T(8,128)(2,1)} %bitcast.21), custom_call_target="tpu_custom_call" | custom-call | bytes 8388608 | tf_op jit(solution)/shard_map/pallas_call | solution.py:139
  78.3 0.0 collective-permute-done.1.refs_2_
  78.3 1.3 %shard_map.49 = (f32[128,512]{1,0:T(8,128)S(1)}, f32[128,512]{1,0:T(8,128)S(1)}) custom-call(bf16[128,4096]{1,0:T(8,128)(2,1)S(1)} %bitcast.15, bf16[64,4096]{1,0:T(8,128)(2,1)S(1)} %collective-permute-done.refs_1_, bf16[64,4096]{1,0:T(8,128)(2,1)S(1)} %collective-permute-done.1.refs_2_, bf16[512,4096]{1,0:T(8,128)(2,1)S(1)} %shard_map.48.refs_3_.refs_4_), custom_call_target="tpu_custom_call" | custom-call | flops 1073741824 | bytes 6291456 | tf_op jit(solution)/shard_map/pallas_call | solution.py:170
  79.6 5.2 %all-gather.2 = f32[256,512]{1,0:T(8,128)S(1)} all-gather(f32[128,512]{1,0:T(8,128)S(1)} %get-tuple-element.19), channel_id=4, replica_groups=mesh['zh'=2,'zl'=4,'yl'=2,'x'=4,'yh'=4,'c'=2] {'c'}, dimensions={0}, use_global_device_ids=true | all-gather | bytes 786432 | tf_op jit(solution)/shard_map/all_gather | solution.py:259
  84.8 0.0 collective-permute-done.2.refs_0_
  84.9 0.0 collective-permute-done.4.refs_2_
  84.9 0.0 collective-permute-done.5.refs_3_
  84.9 1.3 %shard_map.50 = (f32[128,512]{1,0:T(8,128)S(1)}, f32[128,512]{1,0:T(8,128)S(1)}) custom-call(bf16[64,4096]{1,0:T(8,128)(2,1)S(1)} %collective-permute-done.2.refs_0_, bf16[64,4096]{1,0:T(8,128)(2,1)S(1)} %collective-permute-done.3.refs_1_, bf16[64,4096]{1,0:T(8,128)(2,1)S(1)} %collective-permute-done.4.refs_2_, ...), custom_call_target="tpu_custom_call" | custom-call | flops 1073741824 | bytes 6291456 | tf_op jit(solution)/shard_map/pallas_call | solution.py:170
  86.2 4.6 %all-gather.3 = f32[256,512]{1,0:T(8,128)S(1)} all-gather(f32[128,512]{1,0:T(8,128)S(1)} %get-tuple-element.20), channel_id=5, replica_groups=mesh['zh'=2,'zl'=4,'yl'=2,'x'=4,'yh'=4,'c'=2] {'c'}, dimensions={0}, use_global_device_ids=true | all-gather | bytes 786432 | tf_op jit(solution)/shard_map/all_gather | solution.py:261
  90.8 0.1 shard_map.51
  90.9 11.8 %all_to_all.17.parts_ref = bf16[4,4,16,512]{3,2,1,0:T(8,128)(2,1)S(1)} all-to-all(bf16[4,4,16,512]{3,2,1,0:T(8,128)(2,1)S(1)} %bitcast.20), channel_id=1, replica_groups=mesh['zh'=2,'zl'=4,'yl'=2,'x'=4,'yh'=4,'c'=2] {'yh'}, dimensions={0} | all-to-all | bytes 524288 | tf_op jit(solution)/shard_map/all_to_all | solution.py:263
  102.7 0.7 shard_map.52
Async XLA Ops:
  53.9 15.3 %collective-permute-start = (bf16[64,4096]{1,0:T(8,128)(2,1)S(1)}, bf16[64,4096]{1,0:T(8,128)(2,1)S(1)}, u32[]{:S(2)}, u32[]{:S(2)}) collective-permute-start(bf16[64,4096]{1,0:T(8,128)(2,1)S(1)} %bitcast.24), channel_id=1, source_target_pairs={{0,24},{1,9},{2,26},{3,11},{4,28},{5,13},{6,30},{7,15},{8,16},{9,1... | collective-permute-start | bytes 1572872 | tf_op jit(solution)/shard_map/ppermute | solution.py:56
  55.9 18.0 %collective-permute-start.3 = (bf16[64,4096]{1,0:T(8,128)(2,1)S(1)}, bf16[64,4096]{1,0:T(8,128)(2,1)S(1)}, u32[]{:S(2)}, u32[]{:S(2)}) collective-permute-start(bf16[64,4096]{1,0:T(8,128)(2,1)S(1)} %bitcast.26), channel_id=1, source_target_pairs={{0,64},{1,449},{2,66},{3,451},{4,68},{5,453},{6,70},{7,455},{8,72}... | collective-permute-start | bytes 1572872 | tf_op jit(solution)/shard_map/ppermute | solution.py:56
  63.9 14.4 %collective-permute-start.1 = (bf16[64,4096]{1,0:T(8,128)(2,1)S(1)}, bf16[64,4096]{1,0:T(8,128)(2,1)S(1)}, u32[]{:S(2)}, u32[]{:S(2)}) collective-permute-start(bf16[64,4096]{1,0:T(8,128)(2,1)S(1)} %bitcast.27), channel_id=1, source_target_pairs={{0,24},{1,9},{2,26},{3,11},{4,28},{5,13},{6,30},{7,15},{8,16},{9,1... | collective-permute-start | bytes 1572872 | tf_op jit(solution)/shard_map/ppermute | solution.py:56
  67.3 17.6 %collective-permute-start.2 = (bf16[64,4096]{1,0:T(8,128)(2,1)S(1)}, bf16[64,4096]{1,0:T(8,128)(2,1)S(1)}, u32[]{:S(2)}, u32[]{:S(2)}) collective-permute-start(bf16[64,4096]{1,0:T(8,128)(2,1)S(1)} %bitcast.25), channel_id=1, source_target_pairs={{0,64},{1,449},{2,66},{3,451},{4,68},{5,453},{6,70},{7,455},{8,72}... | collective-permute-start | bytes 1572872 | tf_op jit(solution)/shard_map/ppermute | solution.py:56
  69.2 15.6 %collective-permute-start.4 = (bf16[64,4096]{1,0:T(8,128)(2,1)S(1)}, bf16[64,4096]{1,0:T(8,128)(2,1)S(1)}, u32[]{:S(2)}, u32[]{:S(2)}) collective-permute-start(bf16[64,4096]{1,0:T(8,128)(2,1)S(1)} %collective-permute-done.refs_1_), channel_id=1, source_target_pairs={{0,64},{1,449},{2,66},{3,451},{4,68},{5,453},{6,70},{7,455},{8,72}... | collective-permute-start | bytes 1572872 | tf_op jit(solution)/shard_map/ppermute | solution.py:56
  73.8 11.0 %collective-permute-start.5 = (bf16[64,4096]{1,0:T(8,128)(2,1)S(1)}, bf16[64,4096]{1,0:T(8,128)(2,1)S(1)}, u32[]{:S(2)}, u32[]{:S(2)}) collective-permute-start(bf16[64,4096]{1,0:T(8,128)(2,1)S(1)} %collective-permute-done.3.refs_1_), channel_id=1, source_target_pairs={{0,24},{1,9},{2,26},{3,11},{4,28},{5,13},{6,30},{7,15},{8,16},{9,1... | collective-permute-start | bytes 1572872 | tf_op jit(solution)/shard_map/ppermute | solution.py:56

commit v5 on v4

--- a/solution.py
+++ b/solution.py
@@ -40,7 +40,7 @@
         x_pair, z_pair = (x, x ^ near("x", c)[0]), (z, z_neighbour(z, near("z", c)[0]))
         by_parity = lambda pair: sorted(pair, key=lambda at: at % 2)
         corners = [(z2, x2) for z2 in by_parity(z_pair) for x2 in by_parity(x_pair)]
-        groups[tuple(device_index(z2 // 4, z2 % 4, yl, x2, yh, c) for z2, x2 in corners)] = None
+        groups[tuple(device_index(z2 // 4, z2 % 4, y2, x2, yh, c) for z2, x2 in corners for y2 in range(2))] = None
     return [list(group) for group in groups]
 
 
@@ -188,18 +188,19 @@
     for x_base in (x, x ^ x_second):
         for parity in range(2):
             x_of = jnp.where((x_base & 1) == parity, x_base, x_base ^ x_first)
-            places += [(2 * zh + z1) * 4 + x_of for zh in range(2)]
+            places += [((2 * zh + z1) * 4 + x_of, yl) for yl in range(2) for zh in range(2)]
     return places
 
 
 def combine_kernel(keep_0_ref, keep_1_ref, got_0_ref, got_1_ref, out_ref, own_ref, total):
     core = lax.axis_index("c")
     for half, keep_ref in enumerate((keep_0_ref, keep_1_ref)):
-        for block, place in enumerate(block_places(half, core)):
-            total[place] = keep_ref[block * 16 : block * 16 + 16]
+        for block, (place, yl) in enumerate(block_places(half, core)):
+            total[place, yl * 8 : yl * 8 + 8] = keep_ref[block * 8 : block * 8 + 8]
     for half, got_ref in enumerate((got_0_ref, got_1_ref)):
-        for block, place in enumerate(block_places(half, 1 - core)):
-            total[place] = total[place] + got_ref[1 - core, block * 16 : block * 16 + 16]
+        for block, (place, yl) in enumerate(block_places(half, 1 - core)):
+            rows = slice(yl * 8, yl * 8 + 8)
+            total[place, rows] = total[place, rows] + got_ref[1 - core, block * 8 : block * 8 + 8]
     out_ref[...] = total[...].astype(jnp.bfloat16)
     own_ref[...] = total[pl.ds(lax.axis_index("yh") * 4, 4)]
 
@@ -244,11 +245,11 @@
     copies, own, factor = prepare(query_grads, out_inv, in_inv)
     raw = lax.all_gather(lax.all_to_all(copies, "yh", 0, 0, tiled=True), "c")
     pre = precondition(raw, own, factor).reshape(8, 32, 128)
-    pre = lax.all_gather(lax.all_gather(pre, "zh"), "yl", axis=1)
-    held = pre.reshape(32, 4096)
+    pre = lax.all_gather(pre, "zh")
+    held = pre.reshape(16, 4096)
     train = flatten(train_grads.reshape(512, 32, 128))
     square = lax.all_to_all(
-        jnp.broadcast_to(held[None], (4,) + held.shape), NAMES, 0, 0, tiled=True, axis_index_groups=square_groups()
+        jnp.broadcast_to(held[None], (8,) + held.shape), NAMES, 0, 0, tiled=True, axis_index_groups=square_groups()
     ).reshape(128, 4096)
     first, second = square[:64], square[64:]
     x_first, z_second = exchange(first, True), exchange(second, False)

time: 104 us -> 104 us (level)
  blocking collectives: 73.4 us -> 71.2 us
  waiting for transfers between devices: 0.02 us -> 1.39 us
    all_to_all x1, blocking collectives: 14.8 us -> 19.5 us  [body(): lax.all_to_all(jnp.broadcast_to(held[None], (8,) + held.shape), NAMES, 0,...]
    all_gather x2 -> x1, blocking collectives: 16 us -> 11.5 us  [body(): pre = lax.all_gather(pre, 'zh')]
    all_gather x1, blocking collectives: 5.22 us -> 3.33 us  [body(): got_0 = lax.all_gather(send_0, 'c')]
    ppermute x6, waiting for transfers between devices: 0.02 us -> 1.39 us  [exchange(): return lax.ppermute(block, NAMES, step_pairs(along_x))]
  transfers between devices with their start and end apart: 6 -> 6, of which waited for: 0 -> 1; matrix products, arithmetic and copies ran while one was open for 0% -> 0% of each run, Pallas kernels for 4% -> 4%
where the time goes in v5:
time: 104 us; the launch traced here: 103 us
  blocking collectives  71.2 us (68%)
  starting transfers between devices  22.7 us (22%)
  Pallas kernels  7.82 us (8%)
  waiting for transfers between devices  1.39 us (1%)
    ppermute x6, starting transfers between devices, exchange(): return lax.ppermute(block, NAMES, step_pairs(along_x))  22.7 us
    all_to_all x1, blocking collectives, body(): lax.all_to_all(jnp.broadcast_to(held[None], (8,) + held.shape), NAMES, 0,...  19.5 us
    all_to_all x1, blocking collectives, body(): raw = lax.all_gather(lax.all_to_all(copies, 'yh', 0, 0, tiled=True), 'c')  16.4 us
    all_to_all x1, blocking collectives, body(): lax.all_to_all(chip_sum.reshape(4, 4, 16, 512), 'yh', 0, 0, tiled=True)  12 us
    all_gather x1, blocking collectives, body(): pre = lax.all_gather(pre, 'zh')  11.5 us
    all_gather x1, blocking collectives, body(): raw = lax.all_gather(lax.all_to_all(copies, 'yh', 0, 0, tiled=True), 'c')  4.59 us
    all_gather x1, blocking collectives, body(): got_1 = lax.all_gather(send_1, 'c')  3.76 us
    all_gather x1, blocking collectives, body(): got_0 = lax.all_gather(send_0, 'c')  3.33 us
  transfers between devices with their start and end apart: 6, of which 1 were waited for; matrix products, arithmetic and copies ran while one was open for 0% of the time, Pallas kernels for 4%

profile of v5, /device:TPU:1, one launch (start us, length us, event | category | flops | bytes accessed | tf_op | source)
XLA Modules:
  0.0 103.4 jit_solution(10702525472627948165)
XLA Ops:
  0.0 1.1 %shard_map.46 = (bf16[4,8,2,16,128]{4,3,2,1,0:T(8,128)(2,1)S(1)}, f32[2,16,128]{2,1,0:T(8,128)S(1)}, f32[2,128,128]{2,1,0:T(8,128)S(1)}) custom-call(bf16[8,2,16,128]{3,2,1,0:T(8,128)(2,1)} %query_ref.1, f32[2,128,128]{2,1,0:T(8,128)} %out_inv_ref.1, f32[2,128,128]{2,1,0:T(8,128)} %in_inv_ref.1), custom_call_target="tpu_custom_call" | custom-call | bytes 700000 | tf_op jit(solution)/shard_map/pallas_call | solution.py:81
  1.1 16.4 %all_to_all.15 = bf16[4,8,2,16,128]{4,3,2,1,0:T(8,128)(2,1)S(1)} all-to-all(bf16[4,8,2,16,128]{4,3,2,1,0:T(8,128)(2,1)S(1)} %get-tuple-element.14), channel_id=1, replica_groups=mesh['zh'=2,'zl'=4,'yl'=2,'x'=4,'yh'=4,'c'=2] {'yh'}, dimensions={0} | all-to-all | bytes 524288 | tf_op jit(solution)/shard_map/all_to_all | solution.py:246
  17.6 4.6 %all-gather = bf16[8,8,2,16,128]{4,3,2,1,0:T(8,128)(2,1)S(1)} all-gather(bf16[4,8,2,16,128]{4,3,2,1,0:T(8,128)(2,1)S(1)} %all_to_all.15), channel_id=2, replica_groups=mesh['zh'=2,'zl'=4,'yl'=2,'x'=4,'yh'=4,'c'=2] {'c'}, dimensions={0}, use_global_device_ids=true | all-gather | bytes 786432 | tf_op jit(solution)/shard_map/all_gather | solution.py:246
  22.1 0.7 shard_map.47
  22.8 11.5 %all_gather.23 = bf16[2,8,32,128]{3,2,1,0:T(8,128)(2,1)S(1)} all-gather(bf16[1,8,32,128]{3,2,1,0:T(8,128)(2,1)S(1)} %bitcast.19), channel_id=1, replica_groups=mesh['zh'=2,'zl'=4,'yl'=2,'x'=4,'yh'=4,'c'=2] {'zh'}, dimensions={0}, use_global_device_ids=true | all-gather | bytes 196608 | tf_op jit(solution)/shard_map/all_gather | solution.py:248
  34.4 0.1 copy.7
  34.4 0.1 broadcast_in_dim.8
  34.5 19.5 %all_to_all.16 = bf16[8,16,4096]{2,1,0:T(8,128)(2,1)S(1)} all-to-all(bf16[8,16,4096]{2,1,0:T(8,128)(2,1)S(1)} %broadcast_in_dim.8), channel_id=1, replica_groups={{0,32,8,40,448,480,456,488},{1,33,25,57,65,97,89,121},{2,34,10,42,450,4..., dimensions={0} | all-to-all | bytes 2097152 | tf_op jit(solution)/shard_map/all_to_all | solution.py:251
  54.0 0.1 fusion
  54.1 1.9 %collective-permute-start = (bf16[64,4096]{1,0:T(8,128)(2,1)S(1)}, bf16[64,4096]{1,0:T(8,128)(2,1)S(1)}, u32[]{:S(2)}, u32[]{:S(2)}) collective-permute-start(bf16[64,4096]{1,0:T(8,128)(2,1)S(1)} %bitcast.23), channel_id=1, source_target_pairs={{0,24},{1,9},{2,26},{3,11},{4,28},{5,13},{6,30},{7,15},{8,16},{9,1... | collective-permute-start | bytes 1572872 | tf_op jit(solution)/shard_map/ppermute | solution.py:56
  56.0 9.0 %collective-permute-start.3 = (bf16[64,4096]{1,0:T(8,128)(2,1)S(1)}, bf16[64,4096]{1,0:T(8,128)(2,1)S(1)}, u32[]{:S(2)}, u32[]{:S(2)}) collective-permute-start(bf16[64,4096]{1,0:T(8,128)(2,1)S(1)} %bitcast.25), channel_id=1, source_target_pairs={{0,64},{1,449},{2,66},{3,451},{4,68},{5,453},{6,70},{7,455},{8,72}... | collective-permute-start | bytes 1572872 | tf_op jit(solution)/shard_map/ppermute | solution.py:56
  65.0 3.4 %collective-permute-start.1 = (bf16[64,4096]{1,0:T(8,128)(2,1)S(1)}, bf16[64,4096]{1,0:T(8,128)(2,1)S(1)}, u32[]{:S(2)}, u32[]{:S(2)}) collective-permute-start(bf16[64,4096]{1,0:T(8,128)(2,1)S(1)} %bitcast.26), channel_id=1, source_target_pairs={{0,24},{1,9},{2,26},{3,11},{4,28},{5,13},{6,30},{7,15},{8,16},{9,1... | collective-permute-start | bytes 1572872 | tf_op jit(solution)/shard_map/ppermute | solution.py:56
  68.4 1.9 %collective-permute-start.2 = (bf16[64,4096]{1,0:T(8,128)(2,1)S(1)}, bf16[64,4096]{1,0:T(8,128)(2,1)S(1)}, u32[]{:S(2)}, u32[]{:S(2)}) collective-permute-start(bf16[64,4096]{1,0:T(8,128)(2,1)S(1)} %bitcast.24), channel_id=1, source_target_pairs={{0,64},{1,449},{2,66},{3,451},{4,68},{5,453},{6,70},{7,455},{8,72}... | collective-permute-start | bytes 1572872 | tf_op jit(solution)/shard_map/ppermute | solution.py:56
  70.3 0.0 collective-permute-done.refs_1_
  70.3 4.6 %collective-permute-start.4 = (bf16[64,4096]{1,0:T(8,128)(2,1)S(1)}, bf16[64,4096]{1,0:T(8,128)(2,1)S(1)}, u32[]{:S(2)}, u32[]{:S(2)}) collective-permute-start(bf16[64,4096]{1,0:T(8,128)(2,1)S(1)} %collective-permute-done.refs_1_), channel_id=1, source_target_pairs={{0,64},{1,449},{2,66},{3,451},{4,68},{5,453},{6,70},{7,455},{8,72}... | collective-permute-start | bytes 1572872 | tf_op jit(solution)/shard_map/ppermute | solution.py:56
  74.9 0.0 collective-permute-done.3.refs_1_
  74.9 1.9 %collective-permute-start.5 = (bf16[64,4096]{1,0:T(8,128)(2,1)S(1)}, bf16[64,4096]{1,0:T(8,128)(2,1)S(1)}, u32[]{:S(2)}, u32[]{:S(2)}) collective-permute-start(bf16[64,4096]{1,0:T(8,128)(2,1)S(1)} %collective-permute-done.3.refs_1_), channel_id=1, source_target_pairs={{0,24},{1,9},{2,26},{3,11},{4,28},{5,13},{6,30},{7,15},{8,16},{9,1... | collective-permute-start | bytes 1572872 | tf_op jit(solution)/shard_map/ppermute | solution.py:56
  76.8 2.5 %shard_map.48.refs_3_.refs_4_ = bf16[512,4096]{1,0:T(8,128)(2,1)S(1)} custom-call(bf16[512,32,128]{2,1,0:T(8,128)(2,1)} %bitcast.21), custom_call_target="tpu_custom_call" | custom-call | bytes 8388608 | tf_op jit(solution)/shard_map/pallas_call | solution.py:139
  79.3 0.0 collective-permute-done.1.refs_2_
  79.4 1.3 %shard_map.49 = (f32[128,512]{1,0:T(8,128)S(1)}, f32[128,512]{1,0:T(8,128)S(1)}) custom-call(bf16[128,4096]{1,0:T(8,128)(2,1)S(1)} %bitcast.15, bf16[64,4096]{1,0:T(8,128)(2,1)S(1)} %collective-permute-done.refs_1_, bf16[64,4096]{1,0:T(8,128)(2,1)S(1)} %collective-permute-done.1.refs_2_, bf16[512,4096]{1,0:T(8,128)(2,1)S(1)} %shard_map.48.refs_3_.refs_4_), custom_call_target="tpu_custom_call" | custom-call | flops 1073741824 | bytes 6291456 | tf_op jit(solution)/shard_map/pallas_call | solution.py:170
  80.7 3.3 %all-gather.1 = f32[256,512]{1,0:T(8,128)S(1)} all-gather(f32[128,512]{1,0:T(8,128)S(1)} %get-tuple-element.19), channel_id=3, replica_groups=mesh['zh'=2,'zl'=4,'yl'=2,'x'=4,'yh'=4,'c'=2] {'c'}, dimensions={0}, use_global_device_ids=true | all-gather | bytes 786432 | tf_op jit(solution)/shard_map/all_gather | solution.py:260
  84.0 0.0 collective-permute-done.2.refs_0_
  84.0 1.4 %collective-permute-done.4.refs_2_ = bf16[64,4096]{1,0:T(8,128)(2,1)S(1)} collective-permute-done((bf16[64,4096]{1,0:T(8,128)(2,1)S(1)}, bf16[64,4096]{1,0:T(8,128)(2,1)S(1)}, u32[]{:S(2)}, u32[]{:S(2)}) %collective-permute-start.4) | collective-permute-done | bytes 524320 | tf_op jit(solution)/shard_map/ppermute | solution.py:56
  85.4 0.0 collective-permute-done.5.refs_3_
  85.4 1.3 %shard_map.50 = (f32[128,512]{1,0:T(8,128)S(1)}, f32[128,512]{1,0:T(8,128)S(1)}) custom-call(bf16[64,4096]{1,0:T(8,128)(2,1)S(1)} %collective-permute-done.2.refs_0_, bf16[64,4096]{1,0:T(8,128)(2,1)S(1)} %collective-permute-done.3.refs_1_, bf16[64,4096]{1,0:T(8,128)(2,1)S(1)} %collective-permute-done.4.refs_2_, ...), custom_call_target="tpu_custom_call" | custom-call | flops 1073741824 | bytes 6291456 | tf_op jit(solution)/shard_map/pallas_call | solution.py:170
  86.7 3.8 %all-gather.2 = f32[256,512]{1,0:T(8,128)S(1)} all-gather(f32[128,512]{1,0:T(8,128)S(1)} %get-tuple-element.20), channel_id=4, replica_groups=mesh['zh'=2,'zl'=4,'yl'=2,'x'=4,'yh'=4,'c'=2] {'c'}, dimensions={0}, use_global_device_ids=true | all-gather | bytes 786432 | tf_op jit(solution)/shard_map/all_gather | solution.py:262
  90.5 0.1 shard_map.51
  90.7 12.0 %all_to_all.17.parts_ref = bf16[4,4,16,512]{3,2,1,0:T(8,128)(2,1)S(1)} all-to-all(bf16[4,4,16,512]{3,2,1,0:T(8,128)(2,1)S(1)} %bitcast.20), channel_id=1, replica_groups=mesh['zh'=2,'zl'=4,'yl'=2,'x'=4,'yh'=4,'c'=2] {'yh'}, dimensions={0} | all-to-all | bytes 524288 | tf_op jit(solution)/shard_map/all_to_all | solution.py:264
  102.7 0.7 shard_map.52
Async XLA Ops:
  54.1 16.2 %collective-permute-start = (bf16[64,4096]{1,0:T(8,128)(2,1)S(1)}, bf16[64,4096]{1,0:T(8,128)(2,1)S(1)}, u32[]{:S(2)}, u32[]{:S(2)}) collective-permute-start(bf16[64,4096]{1,0:T(8,128)(2,1)S(1)} %bitcast.23), channel_id=1, source_target_pairs={{0,24},{1,9},{2,26},{3,11},{4,28},{5,13},{6,30},{7,15},{8,16},{9,1... | collective-permute-start | bytes 1572872 | tf_op jit(solution)/shard_map/ppermute | solution.py:56
  56.0 18.9 %collective-permute-start.3 = (bf16[64,4096]{1,0:T(8,128)(2,1)S(1)}, bf16[64,4096]{1,0:T(8,128)(2,1)S(1)}, u32[]{:S(2)}, u32[]{:S(2)}) collective-permute-start(bf16[64,4096]{1,0:T(8,128)(2,1)S(1)} %bitcast.25), channel_id=1, source_target_pairs={{0,64},{1,449},{2,66},{3,451},{4,68},{5,453},{6,70},{7,455},{8,72}... | collective-permute-start | bytes 1572872 | tf_op jit(solution)/shard_map/ppermute | solution.py:56
  65.0 14.4 %collective-permute-start.1 = (bf16[64,4096]{1,0:T(8,128)(2,1)S(1)}, bf16[64,4096]{1,0:T(8,128)(2,1)S(1)}, u32[]{:S(2)}, u32[]{:S(2)}) collective-permute-start(bf16[64,4096]{1,0:T(8,128)(2,1)S(1)} %bitcast.26), channel_id=1, source_target_pairs={{0,24},{1,9},{2,26},{3,11},{4,28},{5,13},{6,30},{7,15},{8,16},{9,1... | collective-permute-start | bytes 1572872 | tf_op jit(solution)/shard_map/ppermute | solution.py:56
  68.4 15.7 %collective-permute-start.2 = (bf16[64,4096]{1,0:T(8,128)(2,1)S(1)}, bf16[64,4096]{1,0:T(8,128)(2,1)S(1)}, u32[]{:S(2)}, u32[]{:S(2)}) collective-permute-start(bf16[64,4096]{1,0:T(8,128)(2,1)S(1)} %bitcast.24), channel_id=1, source_target_pairs={{0,64},{1,449},{2,66},{3,451},{4,68},{5,453},{6,70},{7,455},{8,72}... | collective-permute-start | bytes 1572872 | tf_op jit(solution)/shard_map/ppermute | solution.py:56
  70.3 15.1 %collective-permute-start.4 = (bf16[64,4096]{1,0:T(8,128)(2,1)S(1)}, bf16[64,4096]{1,0:T(8,128)(2,1)S(1)}, u32[]{:S(2)}, u32[]{:S(2)}) collective-permute-start(bf16[64,4096]{1,0:T(8,128)(2,1)S(1)} %collective-permute-done.refs_1_), channel_id=1, source_target_pairs={{0,64},{1,449},{2,66},{3,451},{4,68},{5,453},{6,70},{7,455},{8,72}... | collective-permute-start | bytes 1572872 | tf_op jit(solution)/shard_map/ppermute | solution.py:56
  74.9 10.5 %collective-permute-start.5 = (bf16[64,4096]{1,0:T(8,128)(2,1)S(1)}, bf16[64,4096]{1,0:T(8,128)(2,1)S(1)}, u32[]{:S(2)}, u32[]{:S(2)}) collective-permute-start(bf16[64,4096]{1,0:T(8,128)(2,1)S(1)} %collective-permute-done.3.refs_1_), channel_id=1, source_target_pairs={{0,24},{1,9},{2,26},{3,11},{4,28},{5,13},{6,30},{7,15},{8,16},{9,1... | collective-permute-start | bytes 1572872 | tf_op jit(solution)/shard_map/ppermute | solution.py:56

commit v6 on v5

--- a/solution.py
+++ b/solution.py
@@ -15,8 +15,8 @@
 SMALL = pltpu.CompilerParams(vmem_limit_bytes=12 * 1024 * 1024)
 
 
-def near(axis, core):
-    return (1, 3) if (axis == "x") == (core == 0) else (3, 1)
+def near(core):
+    return (3, 1) if core == 0 else (1, 3)
 
 
 def device_index(zh, zl, yl, x, yh, c):
@@ -37,7 +37,7 @@
 def square_groups():
     groups = {}
     for z, yl, x, yh, c in every_device():
-        x_pair, z_pair = (x, x ^ near("x", c)[0]), (z, z_neighbour(z, near("z", c)[0]))
+        x_pair, z_pair = (x, x ^ near(c)[0]), (z, z_neighbour(z, near(c)[0]))
         by_parity = lambda pair: sorted(pair, key=lambda at: at % 2)
         corners = [(z2, x2) for z2 in by_parity(z_pair) for x2 in by_parity(x_pair)]
         groups[tuple(device_index(z2 // 4, z2 % 4, y2, x2, yh, c) for z2, x2 in corners for y2 in range(2))] = None
@@ -47,7 +47,7 @@
 def step_pairs(along_x):
     pairs = []
     for z, yl, x, yh, c in every_device():
-        z2, x2 = (z, x ^ near("x", c)[1]) if along_x else (z_neighbour(z, near("z", c)[1]), x)
+        z2, x2 = (z, x ^ near(c)[1]) if along_x else (z_neighbour(z, near(c)[1]), x)
         pairs.append((device_index(z // 4, z % 4, yl, x, yh, c), device_index(z2 // 4, z2 % 4, yl, x2, yh, c)))
     return pairs
 
@@ -179,15 +179,14 @@
 
 
 def block_places(half, core):
-    x_first, x_second = [jnp.where(core == 0, near("x", 0)[step], near("x", 1)[step]) for step in range(2)]
-    z_first, z_second = [jnp.where(core == 0, near("z", 0)[step], near("z", 1)[step]) for step in range(2)]
+    first, second = [jnp.where(core == 0, near(0)[step], near(1)[step]) for step in range(2)]
     x = lax.axis_index("x")
-    z = lax.axis_index("zl") ^ (z_second if half else 0)
-    z1 = jnp.where((z & 1) == lax.axis_index("c"), z, z ^ z_first) >> 1
+    z = lax.axis_index("zl") ^ (second if half else 0)
+    z1 = jnp.where((z & 1) == lax.axis_index("c"), z, z ^ first) >> 1
     places = []
-    for x_base in (x, x ^ x_second):
+    for x_base in (x, x ^ second):
         for parity in range(2):
-            x_of = jnp.where((x_base & 1) == parity, x_base, x_base ^ x_first)
+            x_of = jnp.where((x_base & 1) == parity, x_base, x_base ^ first)
             places += [((2 * zh + z1) * 4 + x_of, yl) for yl in range(2) for zh in range(2)]
     return places
 

time: 104 us -> 102 us (0.981)
  blocking collectives: 71.2 us -> 67.4 us
  starting transfers between devices: 22.7 us -> 26.2 us
  waiting for transfers between devices: 1.39 us -> 0.02 us
    all_to_all x1, blocking collectives: 19.5 us -> 15.1 us  [body(): lax.all_to_all(jnp.broadcast_to(held[None], (8,) + held.shape), NAMES, 0,...]
    ppermute x6, starting transfers between devices: 22.7 us -> 26.2 us  [exchange(): return lax.ppermute(block, NAMES, step_pairs(along_x))]
    ppermute x6, waiting for transfers between devices: 1.39 us -> 0.02 us  [exchange(): return lax.ppermute(block, NAMES, step_pairs(along_x))]
  transfers between devices with their start and end apart: 6 -> 6, of which waited for: 1 -> 0; matrix products, arithmetic and copies ran while one was open for 0% -> 0% of each run, Pallas kernels for 4% -> 4%
where the time goes in v6:
time: 102 us
  blocking collectives  67.4 us (66%)
  starting transfers between devices  26.2 us (26%)
  Pallas kernels  7.82 us (8%)
    ppermute x6, starting transfers between devices, exchange(): return lax.ppermute(block, NAMES, step_pairs(along_x))  26.2 us
    all_to_all x1, blocking collectives, body(): raw = lax.all_gather(lax.all_to_all(copies, 'yh', 0, 0, tiled=True), 'c')  16.4 us
    all_to_all x1, blocking collectives, body(): lax.all_to_all(jnp.broadcast_to(held[None], (8,) + held.shape), NAMES, 0,...  15.1 us
    all_to_all x1, blocking collectives, body(): lax.all_to_all(chip_sum.reshape(4, 4, 16, 512), 'yh', 0, 0, tiled=True)  12.3 us
    all_gather x1, blocking collectives, body(): pre = lax.all_gather(pre, 'zh')  11.5 us
    all_gather x1, blocking collectives, body(): raw = lax.all_gather(lax.all_to_all(copies, 'yh', 0, 0, tiled=True), 'c')  4.59 us
    all_gather x1, blocking collectives, body(): got_1 = lax.all_gather(send_1, 'c')  3.93 us
    all_gather x1, blocking collectives, body(): got_0 = lax.all_gather(send_0, 'c')  3.48 us
  transfers between devices with their start and end apart: 6, of which 0 were waited for; matrix products, arithmetic and copies ran while one was open for 0% of the time, Pallas kernels for 4%

profile of v6, /device:TPU:1, one launch (start us, length us, event | category | flops | bytes accessed | tf_op | source)
XLA Modules:
  0.0 101.8 jit_solution(4609294808650359801)
XLA Ops:
  0.0 1.1 %shard_map.46 = (bf16[4,8,2,16,128]{4,3,2,1,0:T(8,128)(2,1)S(1)}, f32[2,16,128]{2,1,0:T(8,128)S(1)}, f32[2,128,128]{2,1,0:T(8,128)S(1)}) custom-call(bf16[8,2,16,128]{3,2,1,0:T(8,128)(2,1)} %query_ref.1, f32[2,128,128]{2,1,0:T(8,128)} %out_inv_ref.1, f32[2,128,128]{2,1,0:T(8,128)} %in_inv_ref.1), custom_call_target="tpu_custom_call" | custom-call | bytes 700000 | tf_op jit(solution)/shard_map/pallas_call | solution.py:81
  1.1 16.4 %all_to_all.15 = bf16[4,8,2,16,128]{4,3,2,1,0:T(8,128)(2,1)S(1)} all-to-all(bf16[4,8,2,16,128]{4,3,2,1,0:T(8,128)(2,1)S(1)} %get-tuple-element.14), channel_id=1, replica_groups=mesh['zh'=2,'zl'=4,'yl'=2,'x'=4,'yh'=4,'c'=2] {'yh'}, dimensions={0} | all-to-all | bytes 524288 | tf_op jit(solution)/shard_map/all_to_all | solution.py:245
  17.6 4.6 %all-gather = bf16[8,8,2,16,128]{4,3,2,1,0:T(8,128)(2,1)S(1)} all-gather(bf16[4,8,2,16,128]{4,3,2,1,0:T(8,128)(2,1)S(1)} %all_to_all.15), channel_id=2, replica_groups=mesh['zh'=2,'zl'=4,'yl'=2,'x'=4,'yh'=4,'c'=2] {'c'}, dimensions={0}, use_global_device_ids=true | all-gather | bytes 786432 | tf_op jit(solution)/shard_map/all_gather | solution.py:245
  22.1 0.7 shard_map.47
  22.8 11.5 %all_gather.23 = bf16[2,8,32,128]{3,2,1,0:T(8,128)(2,1)S(1)} all-gather(bf16[1,8,32,128]{3,2,1,0:T(8,128)(2,1)S(1)} %bitcast.19), channel_id=1, replica_groups=mesh['zh'=2,'zl'=4,'yl'=2,'x'=4,'yh'=4,'c'=2] {'zh'}, dimensions={0}, use_global_device_ids=true | all-gather | bytes 196608 | tf_op jit(solution)/shard_map/all_gather | solution.py:247
  34.4 0.1 copy.7
  34.4 0.1 broadcast_in_dim.8
  34.5 15.1 %all_to_all.16 = bf16[8,16,4096]{2,1,0:T(8,128)(2,1)S(1)} all-to-all(bf16[8,16,4096]{2,1,0:T(8,128)(2,1)S(1)} %broadcast_in_dim.8), channel_id=1, replica_groups={{0,32,24,56,448,480,472,504},{1,33,9,41,65,97,73,105},{2,34,26,58,450,4..., dimensions={0} | all-to-all | bytes 2097152 | tf_op jit(solution)/shard_map/all_to_all | solution.py:250
  49.7 0.1 fusion
  49.8 3.7 %collective-permute-start = (bf16[64,4096]{1,0:T(8,128)(2,1)S(1)}, bf16[64,4096]{1,0:T(8,128)(2,1)S(1)}, u32[]{:S(2)}, u32[]{:S(2)}) collective-permute-start(bf16[64,4096]{1,0:T(8,128)(2,1)S(1)} %bitcast.23), channel_id=1, source_target_pairs={{0,8},{1,25},{2,10},{3,27},{4,12},{5,29},{6,14},{7,31},{8,0},{9,17... | collective-permute-start | bytes 1572872 | tf_op jit(solution)/shard_map/ppermute | solution.py:56
  53.5 9.5 %collective-permute-start.3 = (bf16[64,4096]{1,0:T(8,128)(2,1)S(1)}, bf16[64,4096]{1,0:T(8,128)(2,1)S(1)}, u32[]{:S(2)}, u32[]{:S(2)}) collective-permute-start(bf16[64,4096]{1,0:T(8,128)(2,1)S(1)} %bitcast.25), channel_id=1, source_target_pairs={{0,64},{1,449},{2,66},{3,451},{4,68},{5,453},{6,70},{7,455},{8,72}... | collective-permute-start | bytes 1572872 | tf_op jit(solution)/shard_map/ppermute | solution.py:56
  62.9 2.5 %collective-permute-start.1 = (bf16[64,4096]{1,0:T(8,128)(2,1)S(1)}, bf16[64,4096]{1,0:T(8,128)(2,1)S(1)}, u32[]{:S(2)}, u32[]{:S(2)}) collective-permute-start(bf16[64,4096]{1,0:T(8,128)(2,1)S(1)} %bitcast.26), channel_id=1, source_target_pairs={{0,8},{1,25},{2,10},{3,27},{4,12},{5,29},{6,14},{7,31},{8,0},{9,17... | collective-permute-start | bytes 1572872 | tf_op jit(solution)/shard_map/ppermute | solution.py:56
  65.4 1.9 %collective-permute-start.2 = (bf16[64,4096]{1,0:T(8,128)(2,1)S(1)}, bf16[64,4096]{1,0:T(8,128)(2,1)S(1)}, u32[]{:S(2)}, u32[]{:S(2)}) collective-permute-start(bf16[64,4096]{1,0:T(8,128)(2,1)S(1)} %bitcast.24), channel_id=1, source_target_pairs={{0,64},{1,449},{2,66},{3,451},{4,68},{5,453},{6,70},{7,455},{8,72}... | collective-permute-start | bytes 1572872 | tf_op jit(solution)/shard_map/ppermute | solution.py:56
  67.4 0.0 collective-permute-done.refs_1_
  67.4 4.6 %collective-permute-start.4 = (bf16[64,4096]{1,0:T(8,128)(2,1)S(1)}, bf16[64,4096]{1,0:T(8,128)(2,1)S(1)}, u32[]{:S(2)}, u32[]{:S(2)}) collective-permute-start(bf16[64,4096]{1,0:T(8,128)(2,1)S(1)} %collective-permute-done.refs_1_), channel_id=1, source_target_pairs={{0,64},{1,449},{2,66},{3,451},{4,68},{5,453},{6,70},{7,455},{8,72}... | collective-permute-start | bytes 1572872 | tf_op jit(solution)/shard_map/ppermute | solution.py:56
  72.0 0.0 collective-permute-done.3.refs_1_
  72.0 4.0 %collective-permute-start.5 = (bf16[64,4096]{1,0:T(8,128)(2,1)S(1)}, bf16[64,4096]{1,0:T(8,128)(2,1)S(1)}, u32[]{:S(2)}, u32[]{:S(2)}) collective-permute-start(bf16[64,4096]{1,0:T(8,128)(2,1)S(1)} %collective-permute-done.3.refs_1_), channel_id=1, source_target_pairs={{0,8},{1,25},{2,10},{3,27},{4,12},{5,29},{6,14},{7,31},{8,0},{9,17... | collective-permute-start | bytes 1572872 | tf_op jit(solution)/shard_map/ppermute | solution.py:56
  76.0 2.5 %shard_map.48.refs_3_.refs_4_ = bf16[512,4096]{1,0:T(8,128)(2,1)S(1)} custom-call(bf16[512,32,128]{2,1,0:T(8,128)(2,1)} %bitcast.21), custom_call_target="tpu_custom_call" | custom-call | bytes 8388608 | tf_op jit(solution)/shard_map/pallas_call | solution.py:139
  78.5 0.0 collective-permute-done.1.refs_2_
  78.5 1.3 %shard_map.49 = (f32[128,512]{1,0:T(8,128)S(1)}, f32[128,512]{1,0:T(8,128)S(1)}) custom-call(bf16[128,4096]{1,0:T(8,128)(2,1)S(1)} %bitcast.15, bf16[64,4096]{1,0:T(8,128)(2,1)S(1)} %collective-permute-done.refs_1_, bf16[64,4096]{1,0:T(8,128)(2,1)S(1)} %collective-permute-done.1.refs_2_, bf16[512,4096]{1,0:T(8,128)(2,1)S(1)} %shard_map.48.refs_3_.refs_4_), custom_call_target="tpu_custom_call" | custom-call | flops 1073741824 | bytes 6291456 | tf_op jit(solution)/shard_map/pallas_call | solution.py:170
  79.9 3.5 %all-gather.1 = f32[256,512]{1,0:T(8,128)S(1)} all-gather(f32[128,512]{1,0:T(8,128)S(1)} %get-tuple-element.19), channel_id=3, replica_groups=mesh['zh'=2,'zl'=4,'yl'=2,'x'=4,'yh'=4,'c'=2] {'c'}, dimensions={0}, use_global_device_ids=true | all-gather | bytes 786432 | tf_op jit(solution)/shard_map/all_gather | solution.py:259
  83.4 0.0 collective-permute-done.2.refs_0_
  83.4 0.0 collective-permute-done.4.refs_2_
  83.4 0.0 collective-permute-done.5.refs_3_
  83.4 1.3 %shard_map.50 = (f32[128,512]{1,0:T(8,128)S(1)}, f32[128,512]{1,0:T(8,128)S(1)}) custom-call(bf16[64,4096]{1,0:T(8,128)(2,1)S(1)} %collective-permute-done.2.refs_0_, bf16[64,4096]{1,0:T(8,128)(2,1)S(1)} %collective-permute-done.3.refs_1_, bf16[64,4096]{1,0:T(8,128)(2,1)S(1)} %collective-permute-done.4.refs_2_, ...), custom_call_target="tpu_custom_call" | custom-call | flops 1073741824 | bytes 6291456 | tf_op jit(solution)/shard_map/pallas_call | solution.py:170
  84.7 3.9 %all-gather.2 = f32[256,512]{1,0:T(8,128)S(1)} all-gather(f32[128,512]{1,0:T(8,128)S(1)} %get-tuple-element.20), channel_id=4, replica_groups=mesh['zh'=2,'zl'=4,'yl'=2,'x'=4,'yh'=4,'c'=2] {'c'}, dimensions={0}, use_global_device_ids=true | all-gather | bytes 786432 | tf_op jit(solution)/shard_map/all_gather | solution.py:261
  88.6 0.1 shard_map.51
  88.8 12.3 %all_to_all.17.parts_ref = bf16[4,4,16,512]{3,2,1,0:T(8,128)(2,1)S(1)} all-to-all(bf16[4,4,16,512]{3,2,1,0:T(8,128)(2,1)S(1)} %bitcast.20), channel_id=1, replica_groups=mesh['zh'=2,'zl'=4,'yl'=2,'x'=4,'yh'=4,'c'=2] {'yh'}, dimensions={0} | all-to-all | bytes 524288 | tf_op jit(solution)/shard_map/all_to_all | solution.py:263
  101.1 0.7 shard_map.52
Async XLA Ops:
  49.8 17.6 %collective-permute-start = (bf16[64,4096]{1,0:T(8,128)(2,1)S(1)}, bf16[64,4096]{1,0:T(8,128)(2,1)S(1)}, u32[]{:S(2)}, u32[]{:S(2)}) collective-permute-start(bf16[64,4096]{1,0:T(8,128)(2,1)S(1)} %bitcast.23), channel_id=1, source_target_pairs={{0,8},{1,25},{2,10},{3,27},{4,12},{5,29},{6,14},{7,31},{8,0},{9,17... | collective-permute-start | bytes 1572872 | tf_op jit(solution)/shard_map/ppermute | solution.py:56
  53.5 18.5 %collective-permute-start.3 = (bf16[64,4096]{1,0:T(8,128)(2,1)S(1)}, bf16[64,4096]{1,0:T(8,128)(2,1)S(1)}, u32[]{:S(2)}, u32[]{:S(2)}) collective-permute-start(bf16[64,4096]{1,0:T(8,128)(2,1)S(1)} %bitcast.25), channel_id=1, source_target_pairs={{0,64},{1,449},{2,66},{3,451},{4,68},{5,453},{6,70},{7,455},{8,72}... | collective-permute-start | bytes 1572872 | tf_op jit(solution)/shard_map/ppermute | solution.py:56
  62.9 15.6 %collective-permute-start.1 = (bf16[64,4096]{1,0:T(8,128)(2,1)S(1)}, bf16[64,4096]{1,0:T(8,128)(2,1)S(1)}, u32[]{:S(2)}, u32[]{:S(2)}) collective-permute-start(bf16[64,4096]{1,0:T(8,128)(2,1)S(1)} %bitcast.26), channel_id=1, source_target_pairs={{0,8},{1,25},{2,10},{3,27},{4,12},{5,29},{6,14},{7,31},{8,0},{9,17... | collective-permute-start | bytes 1572872 | tf_op jit(solution)/shard_map/ppermute | solution.py:56
  65.4 17.9 %collective-permute-start.2 = (bf16[64,4096]{1,0:T(8,128)(2,1)S(1)}, bf16[64,4096]{1,0:T(8,128)(2,1)S(1)}, u32[]{:S(2)}, u32[]{:S(2)}) collective-permute-start(bf16[64,4096]{1,0:T(8,128)(2,1)S(1)} %bitcast.24), channel_id=1, source_target_pairs={{0,64},{1,449},{2,66},{3,451},{4,68},{5,453},{6,70},{7,455},{8,72}... | collective-permute-start | bytes 1572872 | tf_op jit(solution)/shard_map/ppermute | solution.py:56
  67.4 16.0 %collective-permute-start.4 = (bf16[64,4096]{1,0:T(8,128)(2,1)S(1)}, bf16[64,4096]{1,0:T(8,128)(2,1)S(1)}, u32[]{:S(2)}, u32[]{:S(2)}) collective-permute-start(bf16[64,4096]{1,0:T(8,128)(2,1)S(1)} %collective-permute-done.refs_1_), channel_id=1, source_target_pairs={{0,64},{1,449},{2,66},{3,451},{4,68},{5,453},{6,70},{7,455},{8,72}... | collective-permute-start | bytes 1572872 | tf_op jit(solution)/shard_map/ppermute | solution.py:56
  72.0 11.4 %collective-permute-start.5 = (bf16[64,4096]{1,0:T(8,128)(2,1)S(1)}, bf16[64,4096]{1,0:T(8,128)(2,1)S(1)}, u32[]{:S(2)}, u32[]{:S(2)}) collective-permute-start(bf16[64,4096]{1,0:T(8,128)(2,1)S(1)} %collective-permute-done.3.refs_1_), channel_id=1, source_target_pairs={{0,8},{1,25},{2,10},{3,27},{4,12},{5,29},{6,14},{7,31},{8,0},{9,17... | collective-permute-start | bytes 1572872 | tf_op jit(solution)/shard_map/ppermute | solution.py:56

commit v7 on v6

--- a/solution.py
+++ b/solution.py
@@ -251,9 +251,9 @@
         jnp.broadcast_to(held[None], (8,) + held.shape), NAMES, 0, 0, tiled=True, axis_index_groups=square_groups()
     ).reshape(128, 4096)
     first, second = square[:64], square[64:]
-    x_first, z_second = exchange(first, True), exchange(second, False)
-    x_second, z_first = exchange(second, True), exchange(first, False)
-    both_first, both_second = exchange(x_first, False), exchange(z_second, True)
+    z_first, x_second = exchange(first, False), exchange(second, True)
+    z_second, x_first = exchange(second, False), exchange(first, True)
+    both_first, both_second = exchange(z_first, True), exchange(x_second, False)
 
     keep_0, send_0 = half_scores((square, x_first, x_second), train)
     got_0 = lax.all_gather(send_0, "c")

time: 102 us -> 102 us (level)
  no operation moved by 1% of the time
where the time goes in v7:
time: 102 us
  blocking collectives  67.4 us (66%)
  starting transfers between devices  26.2 us (26%)
  Pallas kernels  7.82 us (8%)
    ppermute x6, starting transfers between devices, exchange(): return lax.ppermute(block, NAMES, step_pairs(along_x))  26.2 us
    all_to_all x1, blocking collectives, body(): raw = lax.all_gather(lax.all_to_all(copies, 'yh', 0, 0, tiled=True), 'c')  16.4 us
    all_to_all x1, blocking collectives, body(): lax.all_to_all(jnp.broadcast_to(held[None], (8,) + held.shape), NAMES, 0,...  15.1 us
    all_to_all x1, blocking collectives, body(): lax.all_to_all(chip_sum.reshape(4, 4, 16, 512), 'yh', 0, 0, tiled=True)  12.3 us
    all_gather x1, blocking collectives, body(): pre = lax.all_gather(pre, 'zh')  11.5 us
    all_gather x1, blocking collectives, body(): raw = lax.all_gather(lax.all_to_all(copies, 'yh', 0, 0, tiled=True), 'c')  4.59 us
    all_gather x1, blocking collectives, body(): got_1 = lax.all_gather(send_1, 'c')  3.93 us
    all_gather x1, blocking collectives, body(): got_0 = lax.all_gather(send_0, 'c')  3.44 us
  transfers between devices with their start and end apart: 6, of which 0 were waited for; matrix products, arithmetic and copies ran while one was open for 0% of the time, Pallas kernels for 4%

profile of v7, /device:TPU:1, one launch (start us, length us, event | category | flops | bytes accessed | tf_op | source)
XLA Modules:
  0.0 101.7 jit_solution(2675287170833241974)
XLA Ops:
  0.0 1.1 %shard_map.46 = (bf16[4,8,2,16,128]{4,3,2,1,0:T(8,128)(2,1)S(1)}, f32[2,16,128]{2,1,0:T(8,128)S(1)}, f32[2,128,128]{2,1,0:T(8,128)S(1)}) custom-call(bf16[8,2,16,128]{3,2,1,0:T(8,128)(2,1)} %query_ref.1, f32[2,128,128]{2,1,0:T(8,128)} %out_inv_ref.1, f32[2,128,128]{2,1,0:T(8,128)} %in_inv_ref.1), custom_call_target="tpu_custom_call" | custom-call | bytes 700000 | tf_op jit(solution)/shard_map/pallas_call | solution.py:81
  1.1 16.4 %all_to_all.15 = bf16[4,8,2,16,128]{4,3,2,1,0:T(8,128)(2,1)S(1)} all-to-all(bf16[4,8,2,16,128]{4,3,2,1,0:T(8,128)(2,1)S(1)} %get-tuple-element.14), channel_id=1, replica_groups=mesh['zh'=2,'zl'=4,'yl'=2,'x'=4,'yh'=4,'c'=2] {'yh'}, dimensions={0} | all-to-all | bytes 524288 | tf_op jit(solution)/shard_map/all_to_all | solution.py:245
  17.6 4.6 %all-gather = bf16[8,8,2,16,128]{4,3,2,1,0:T(8,128)(2,1)S(1)} all-gather(bf16[4,8,2,16,128]{4,3,2,1,0:T(8,128)(2,1)S(1)} %all_to_all.15), channel_id=2, replica_groups=mesh['zh'=2,'zl'=4,'yl'=2,'x'=4,'yh'=4,'c'=2] {'c'}, dimensions={0}, use_global_device_ids=true | all-gather | bytes 786432 | tf_op jit(solution)/shard_map/all_gather | solution.py:245
  22.1 0.7 shard_map.47
  22.8 11.5 %all_gather.23 = bf16[2,8,32,128]{3,2,1,0:T(8,128)(2,1)S(1)} all-gather(bf16[1,8,32,128]{3,2,1,0:T(8,128)(2,1)S(1)} %bitcast.19), channel_id=1, replica_groups=mesh['zh'=2,'zl'=4,'yl'=2,'x'=4,'yh'=4,'c'=2] {'zh'}, dimensions={0}, use_global_device_ids=true | all-gather | bytes 196608 | tf_op jit(solution)/shard_map/all_gather | solution.py:247
  34.4 0.1 copy.7
  34.4 0.1 broadcast_in_dim.8
  34.5 15.1 %all_to_all.16 = bf16[8,16,4096]{2,1,0:T(8,128)(2,1)S(1)} all-to-all(bf16[8,16,4096]{2,1,0:T(8,128)(2,1)S(1)} %broadcast_in_dim.8), channel_id=1, replica_groups={{0,32,24,56,448,480,472,504},{1,33,9,41,65,97,73,105},{2,34,26,58,450,4..., dimensions={0} | all-to-all | bytes 2097152 | tf_op jit(solution)/shard_map/all_to_all | solution.py:250
  49.7 0.1 fusion
  49.8 9.2 %collective-permute-start.2 = (bf16[64,4096]{1,0:T(8,128)(2,1)S(1)}, bf16[64,4096]{1,0:T(8,128)(2,1)S(1)}, u32[]{:S(2)}, u32[]{:S(2)}) collective-permute-start(bf16[64,4096]{1,0:T(8,128)(2,1)S(1)} %bitcast.25), channel_id=1, source_target_pairs={{0,64},{1,449},{2,66},{3,451},{4,68},{5,453},{6,70},{7,455},{8,72}... | collective-permute-start | bytes 1572872 | tf_op jit(solution)/shard_map/ppermute | solution.py:56
  58.9 4.0 %collective-permute-start.1 = (bf16[64,4096]{1,0:T(8,128)(2,1)S(1)}, bf16[64,4096]{1,0:T(8,128)(2,1)S(1)}, u32[]{:S(2)}, u32[]{:S(2)}) collective-permute-start(bf16[64,4096]{1,0:T(8,128)(2,1)S(1)} %bitcast.23), channel_id=1, source_target_pairs={{0,8},{1,25},{2,10},{3,27},{4,12},{5,29},{6,14},{7,31},{8,0},{9,17... | collective-permute-start | bytes 1572872 | tf_op jit(solution)/shard_map/ppermute | solution.py:56
  62.9 2.5 %collective-permute-start = (bf16[64,4096]{1,0:T(8,128)(2,1)S(1)}, bf16[64,4096]{1,0:T(8,128)(2,1)S(1)}, u32[]{:S(2)}, u32[]{:S(2)}) collective-permute-start(bf16[64,4096]{1,0:T(8,128)(2,1)S(1)} %bitcast.26), channel_id=1, source_target_pairs={{0,8},{1,25},{2,10},{3,27},{4,12},{5,29},{6,14},{7,31},{8,0},{9,17... | collective-permute-start | bytes 1572872 | tf_op jit(solution)/shard_map/ppermute | solution.py:56
  65.4 1.9 %collective-permute-start.3 = (bf16[64,4096]{1,0:T(8,128)(2,1)S(1)}, bf16[64,4096]{1,0:T(8,128)(2,1)S(1)}, u32[]{:S(2)}, u32[]{:S(2)}) collective-permute-start(bf16[64,4096]{1,0:T(8,128)(2,1)S(1)} %bitcast.24), channel_id=1, source_target_pairs={{0,64},{1,449},{2,66},{3,451},{4,68},{5,453},{6,70},{7,455},{8,72}... | collective-permute-start | bytes 1572872 | tf_op jit(solution)/shard_map/ppermute | solution.py:56
  67.4 0.0 collective-permute-done.2.refs_0_
  67.4 4.0 %collective-permute-start.4 = (bf16[64,4096]{1,0:T(8,128)(2,1)S(1)}, bf16[64,4096]{1,0:T(8,128)(2,1)S(1)}, u32[]{:S(2)}, u32[]{:S(2)}) collective-permute-start(bf16[64,4096]{1,0:T(8,128)(2,1)S(1)} %collective-permute-done.2.refs_0_), channel_id=1, source_target_pairs={{0,8},{1,25},{2,10},{3,27},{4,12},{5,29},{6,14},{7,31},{8,0},{9,17... | collective-permute-start | bytes 1572872 | tf_op jit(solution)/shard_map/ppermute | solution.py:56
  71.4 0.0 collective-permute-done.1.refs_2_
  71.4 4.6 %collective-permute-start.5 = (bf16[64,4096]{1,0:T(8,128)(2,1)S(1)}, bf16[64,4096]{1,0:T(8,128)(2,1)S(1)}, u32[]{:S(2)}, u32[]{:S(2)}) collective-permute-start(bf16[64,4096]{1,0:T(8,128)(2,1)S(1)} %collective-permute-done.1.refs_2_), channel_id=1, source_target_pairs={{0,64},{1,449},{2,66},{3,451},{4,68},{5,453},{6,70},{7,455},{8,72}... | collective-permute-start | bytes 1572872 | tf_op jit(solution)/shard_map/ppermute | solution.py:56
  76.0 2.5 %shard_map.48.refs_3_.refs_4_ = bf16[512,4096]{1,0:T(8,128)(2,1)S(1)} custom-call(bf16[512,32,128]{2,1,0:T(8,128)(2,1)} %bitcast.21), custom_call_target="tpu_custom_call" | custom-call | bytes 8388608 | tf_op jit(solution)/shard_map/pallas_call | solution.py:139
  78.5 0.0 collective-permute-done.refs_1_
  78.5 1.3 %shard_map.49 = (f32[128,512]{1,0:T(8,128)S(1)}, f32[128,512]{1,0:T(8,128)S(1)}) custom-call(bf16[128,4096]{1,0:T(8,128)(2,1)S(1)} %bitcast.15, bf16[64,4096]{1,0:T(8,128)(2,1)S(1)} %collective-permute-done.refs_1_, bf16[64,4096]{1,0:T(8,128)(2,1)S(1)} %collective-permute-done.1.refs_2_, bf16[512,4096]{1,0:T(8,128)(2,1)S(1)} %shard_map.48.refs_3_.refs_4_), custom_call_target="tpu_custom_call" | custom-call | flops 1073741824 | bytes 6291456 | tf_op jit(solution)/shard_map/pallas_call | solution.py:170
  79.9 3.4 %all-gather.1 = f32[256,512]{1,0:T(8,128)S(1)} all-gather(f32[128,512]{1,0:T(8,128)S(1)} %get-tuple-element.19), channel_id=3, replica_groups=mesh['zh'=2,'zl'=4,'yl'=2,'x'=4,'yh'=4,'c'=2] {'c'}, dimensions={0}, use_global_device_ids=true | all-gather | bytes 786432 | tf_op jit(solution)/shard_map/all_gather | solution.py:259
  83.3 0.0 collective-permute-done.3.refs_1_
  83.3 0.0 collective-permute-done.4.refs_2_
  83.3 0.0 collective-permute-done.5.refs_3_
  83.3 1.3 %shard_map.50 = (f32[128,512]{1,0:T(8,128)S(1)}, f32[128,512]{1,0:T(8,128)S(1)}) custom-call(bf16[64,4096]{1,0:T(8,128)(2,1)S(1)} %collective-permute-done.2.refs_0_, bf16[64,4096]{1,0:T(8,128)(2,1)S(1)} %collective-permute-done.3.refs_1_, bf16[64,4096]{1,0:T(8,128)(2,1)S(1)} %collective-permute-done.4.refs_2_, ...), custom_call_target="tpu_custom_call" | custom-call | flops 1073741824 | bytes 6291456 | tf_op jit(solution)/shard_map/pallas_call | solution.py:170
  84.7 3.9 %all-gather.2 = f32[256,512]{1,0:T(8,128)S(1)} all-gather(f32[128,512]{1,0:T(8,128)S(1)} %get-tuple-element.20), channel_id=4, replica_groups=mesh['zh'=2,'zl'=4,'yl'=2,'x'=4,'yh'=4,'c'=2] {'c'}, dimensions={0}, use_global_device_ids=true | all-gather | bytes 786432 | tf_op jit(solution)/shard_map/all_gather | solution.py:261
  88.6 0.1 shard_map.51
  88.7 12.3 %all_to_all.17.parts_ref = bf16[4,4,16,512]{3,2,1,0:T(8,128)(2,1)S(1)} all-to-all(bf16[4,4,16,512]{3,2,1,0:T(8,128)(2,1)S(1)} %bitcast.20), channel_id=1, replica_groups=mesh['zh'=2,'zl'=4,'yl'=2,'x'=4,'yh'=4,'c'=2] {'yh'}, dimensions={0} | all-to-all | bytes 524288 | tf_op jit(solution)/shard_map/all_to_all | solution.py:263
  101.0 0.7 shard_map.52
Async XLA Ops:
  49.8 17.6 %collective-permute-start.2 = (bf16[64,4096]{1,0:T(8,128)(2,1)S(1)}, bf16[64,4096]{1,0:T(8,128)(2,1)S(1)}, u32[]{:S(2)}, u32[]{:S(2)}) collective-permute-start(bf16[64,4096]{1,0:T(8,128)(2,1)S(1)} %bitcast.25), channel_id=1, source_target_pairs={{0,64},{1,449},{2,66},{3,451},{4,68},{5,453},{6,70},{7,455},{8,72}... | collective-permute-start | bytes 1572872 | tf_op jit(solution)/shard_map/ppermute | solution.py:56
  58.9 12.5 %collective-permute-start.1 = (bf16[64,4096]{1,0:T(8,128)(2,1)S(1)}, bf16[64,4096]{1,0:T(8,128)(2,1)S(1)}, u32[]{:S(2)}, u32[]{:S(2)}) collective-permute-start(bf16[64,4096]{1,0:T(8,128)(2,1)S(1)} %bitcast.23), channel_id=1, source_target_pairs={{0,8},{1,25},{2,10},{3,27},{4,12},{5,29},{6,14},{7,31},{8,0},{9,17... | collective-permute-start | bytes 1572872 | tf_op jit(solution)/shard_map/ppermute | solution.py:56
  62.9 15.6 %collective-permute-start = (bf16[64,4096]{1,0:T(8,128)(2,1)S(1)}, bf16[64,4096]{1,0:T(8,128)(2,1)S(1)}, u32[]{:S(2)}, u32[]{:S(2)}) collective-permute-start(bf16[64,4096]{1,0:T(8,128)(2,1)S(1)} %bitcast.26), channel_id=1, source_target_pairs={{0,8},{1,25},{2,10},{3,27},{4,12},{5,29},{6,14},{7,31},{8,0},{9,17... | collective-permute-start | bytes 1572872 | tf_op jit(solution)/shard_map/ppermute | solution.py:56
  65.4 17.9 %collective-permute-start.3 = (bf16[64,4096]{1,0:T(8,128)(2,1)S(1)}, bf16[64,4096]{1,0:T(8,128)(2,1)S(1)}, u32[]{:S(2)}, u32[]{:S(2)}) collective-permute-start(bf16[64,4096]{1,0:T(8,128)(2,1)S(1)} %bitcast.24), channel_id=1, source_target_pairs={{0,64},{1,449},{2,66},{3,451},{4,68},{5,453},{6,70},{7,455},{8,72}... | collective-permute-start | bytes 1572872 | tf_op jit(solution)/shard_map/ppermute | solution.py:56
  67.4 15.9 %collective-permute-start.4 = (bf16[64,4096]{1,0:T(8,128)(2,1)S(1)}, bf16[64,4096]{1,0:T(8,128)(2,1)S(1)}, u32[]{:S(2)}, u32[]{:S(2)}) collective-permute-start(bf16[64,4096]{1,0:T(8,128)(2,1)S(1)} %collective-permute-done.2.refs_0_), channel_id=1, source_target_pairs={{0,8},{1,25},{2,10},{3,27},{4,12},{5,29},{6,14},{7,31},{8,0},{9,17... | collective-permute-start | bytes 1572872 | tf_op jit(solution)/shard_map/ppermute | solution.py:56
  71.4 11.9 %collective-permute-start.5 = (bf16[64,4096]{1,0:T(8,128)(2,1)S(1)}, bf16[64,4096]{1,0:T(8,128)(2,1)S(1)}, u32[]{:S(2)}, u32[]{:S(2)}) collective-permute-start(bf16[64,4096]{1,0:T(8,128)(2,1)S(1)} %collective-permute-done.1.refs_2_), channel_id=1, source_target_pairs={{0,64},{1,449},{2,66},{3,451},{4,68},{5,453},{6,70},{7,455},{8,72}... | collective-permute-start | bytes 1572872 | tf_op jit(solution)/shard_map/ppermute | solution.py:56

commit v8 on v7

--- a/solution.py
+++ b/solution.py
@@ -44,16 +44,17 @@
     return [list(group) for group in groups]
 
 
-def step_pairs(along_x):
+def step_pairs(way):
     pairs = []
     for z, yl, x, yh, c in every_device():
+        along_x = way == c
         z2, x2 = (z, x ^ near(c)[1]) if along_x else (z_neighbour(z, near(c)[1]), x)
         pairs.append((device_index(z // 4, z % 4, yl, x, yh, c), device_index(z2 // 4, z2 % 4, yl, x2, yh, c)))
     return pairs
 
 
-def exchange(block, along_x):
-    return lax.ppermute(block, NAMES, step_pairs(along_x))
+def exchange(block, way):
+    return lax.ppermute(block, NAMES, step_pairs(way))
 
 
 def three_parts(value):
@@ -180,11 +181,12 @@
 
 def block_places(half, core):
     first, second = [jnp.where(core == 0, near(0)[step], near(1)[step]) for step in range(2)]
-    x = lax.axis_index("x")
-    z = lax.axis_index("zl") ^ (second if half else 0)
-    z1 = jnp.where((z & 1) == lax.axis_index("c"), z, z ^ first) >> 1
+    x, z = lax.axis_index("x"), lax.axis_index("zl")
     places = []
-    for x_base in (x, x ^ second):
+    for piece in range(2):
+        x_far, z_far = jnp.where(core == 0, piece, half), jnp.where(core == 0, half, piece)
+        x_base, z_base = x ^ (second * x_far), z ^ (second * z_far)
+        z1 = jnp.where((z_base & 1) == lax.axis_index("c"), z_base, z_base ^ first) >> 1
         for parity in range(2):
             x_of = jnp.where((x_base & 1) == parity, x_base, x_base ^ first)
             places += [((2 * zh + z1) * 4 + x_of, yl) for yl in range(2) for zh in range(2)]
@@ -251,9 +253,9 @@
         jnp.broadcast_to(held[None], (8,) + held.shape), NAMES, 0, 0, tiled=True, axis_index_groups=square_groups()
     ).reshape(128, 4096)
     first, second = square[:64], square[64:]
-    z_first, x_second = exchange(first, False), exchange(second, True)
-    z_second, x_first = exchange(second, False), exchange(first, True)
-    both_first, both_second = exchange(z_first, True), exchange(x_second, False)
+    x_first, z_second = exchange(first, 0), exchange(second, 1)
+    x_second, z_first = exchange(second, 0), exchange(first, 1)
+    both_first, both_second = exchange(x_first, 1), exchange(z_second, 0)
 
     keep_0, send_0 = half_scores((square, x_first, x_second), train)
     got_0 = lax.all_gather(send_0, "c")

time: 102 us -> 102 us (level)
  no operation moved by 1% of the time
where the time goes in v8:
time: 102 us
  blocking collectives  67.4 us (66%)
  starting transfers between devices  26.2 us (26%)
  Pallas kernels  7.82 us (8%)
    ppermute x6, starting transfers between devices, exchange(): return lax.ppermute(block, NAMES, step_pairs(way))  26.2 us
    all_to_all x1, blocking collectives, body(): raw = lax.all_gather(lax.all_to_all(copies, 'yh', 0, 0, tiled=True), 'c')  16.4 us
    all_to_all x1, blocking collectives, body(): lax.all_to_all(jnp.broadcast_to(held[None], (8,) + held.shape), NAMES, 0,...  15.1 us
    all_to_all x1, blocking collectives, body(): lax.all_to_all(chip_sum.reshape(4, 4, 16, 512), 'yh', 0, 0, tiled=True)  12.3 us
    all_gather x1, blocking collectives, body(): pre = lax.all_gather(pre, 'zh')  11.5 us
    all_gather x1, blocking collectives, body(): raw = lax.all_gather(lax.all_to_all(copies, 'yh', 0, 0, tiled=True), 'c')  4.59 us
    all_gather x1, blocking collectives, body(): got_1 = lax.all_gather(send_1, 'c')  3.93 us
    all_gather x1, blocking collectives, body(): got_0 = lax.all_gather(send_0, 'c')  3.44 us
  transfers between devices with their start and end apart: 6, of which 0 were waited for; matrix products, arithmetic and copies ran while one was open for 0% of the time, Pallas kernels for 4%

profile of v8, /device:TPU:1, one launch (start us, length us, event | category | flops | bytes accessed | tf_op | source)
XLA Modules:
  0.0 101.7 jit_solution(7024291130820487232)
XLA Ops:
  0.0 1.1 %shard_map.46 = (bf16[4,8,2,16,128]{4,3,2,1,0:T(8,128)(2,1)S(1)}, f32[2,16,128]{2,1,0:T(8,128)S(1)}, f32[2,128,128]{2,1,0:T(8,128)S(1)}) custom-call(bf16[8,2,16,128]{3,2,1,0:T(8,128)(2,1)} %query_ref.1, f32[2,128,128]{2,1,0:T(8,128)} %out_inv_ref.1, f32[2,128,128]{2,1,0:T(8,128)} %in_inv_ref.1), custom_call_target="tpu_custom_call" | custom-call | bytes 700000 | tf_op jit(solution)/shard_map/pallas_call | solution.py:82
  1.1 16.4 %all_to_all.15 = bf16[4,8,2,16,128]{4,3,2,1,0:T(8,128)(2,1)S(1)} all-to-all(bf16[4,8,2,16,128]{4,3,2,1,0:T(8,128)(2,1)S(1)} %get-tuple-element.14), channel_id=1, replica_groups=mesh['zh'=2,'zl'=4,'yl'=2,'x'=4,'yh'=4,'c'=2] {'yh'}, dimensions={0} | all-to-all | bytes 524288 | tf_op jit(solution)/shard_map/all_to_all | solution.py:247
  17.6 4.6 %all-gather = bf16[8,8,2,16,128]{4,3,2,1,0:T(8,128)(2,1)S(1)} all-gather(bf16[4,8,2,16,128]{4,3,2,1,0:T(8,128)(2,1)S(1)} %all_to_all.15), channel_id=2, replica_groups=mesh['zh'=2,'zl'=4,'yl'=2,'x'=4,'yh'=4,'c'=2] {'c'}, dimensions={0}, use_global_device_ids=true | all-gather | bytes 786432 | tf_op jit(solution)/shard_map/all_gather | solution.py:247
  22.1 0.7 shard_map.47
  22.8 11.5 %all_gather.23 = bf16[2,8,32,128]{3,2,1,0:T(8,128)(2,1)S(1)} all-gather(bf16[1,8,32,128]{3,2,1,0:T(8,128)(2,1)S(1)} %bitcast.19), channel_id=1, replica_groups=mesh['zh'=2,'zl'=4,'yl'=2,'x'=4,'yh'=4,'c'=2] {'zh'}, dimensions={0}, use_global_device_ids=true | all-gather | bytes 196608 | tf_op jit(solution)/shard_map/all_gather | solution.py:249
  34.4 0.1 copy.7
  34.4 0.1 broadcast_in_dim.8
  34.5 15.1 %all_to_all.16 = bf16[8,16,4096]{2,1,0:T(8,128)(2,1)S(1)} all-to-all(bf16[8,16,4096]{2,1,0:T(8,128)(2,1)S(1)} %broadcast_in_dim.8), channel_id=1, replica_groups={{0,32,24,56,448,480,472,504},{1,33,9,41,65,97,73,105},{2,34,26,58,450,4..., dimensions={0} | all-to-all | bytes 2097152 | tf_op jit(solution)/shard_map/all_to_all | solution.py:252
  49.7 0.1 fusion
  49.8 9.2 %collective-permute-start = (bf16[64,4096]{1,0:T(8,128)(2,1)S(1)}, bf16[64,4096]{1,0:T(8,128)(2,1)S(1)}, u32[]{:S(2)}, u32[]{:S(2)}) collective-permute-start(bf16[64,4096]{1,0:T(8,128)(2,1)S(1)} %bitcast.23), channel_id=1, source_target_pairs={{0,8},{1,449},{2,10},{3,451},{4,12},{5,453},{6,14},{7,455},{8,0},{... | collective-permute-start | bytes 1572872 | tf_op jit(solution)/shard_map/ppermute | solution.py:57
  58.9 4.0 %collective-permute-start.3 = (bf16[64,4096]{1,0:T(8,128)(2,1)S(1)}, bf16[64,4096]{1,0:T(8,128)(2,1)S(1)}, u32[]{:S(2)}, u32[]{:S(2)}) collective-permute-start(bf16[64,4096]{1,0:T(8,128)(2,1)S(1)} %bitcast.25), channel_id=1, source_target_pairs={{0,64},{1,25},{2,66},{3,27},{4,68},{5,29},{6,70},{7,31},{8,72},{9,... | collective-permute-start | bytes 1572872 | tf_op jit(solution)/shard_map/ppermute | solution.py:57
  62.9 1.9 %collective-permute-start.1 = (bf16[64,4096]{1,0:T(8,128)(2,1)S(1)}, bf16[64,4096]{1,0:T(8,128)(2,1)S(1)}, u32[]{:S(2)}, u32[]{:S(2)}) collective-permute-start(bf16[64,4096]{1,0:T(8,128)(2,1)S(1)} %bitcast.26), channel_id=1, source_target_pairs={{0,8},{1,449},{2,10},{3,451},{4,12},{5,453},{6,14},{7,455},{8,0},{... | collective-permute-start | bytes 1572872 | tf_op jit(solution)/shard_map/ppermute | solution.py:57
  64.9 2.5 %collective-permute-start.2 = (bf16[64,4096]{1,0:T(8,128)(2,1)S(1)}, bf16[64,4096]{1,0:T(8,128)(2,1)S(1)}, u32[]{:S(2)}, u32[]{:S(2)}) collective-permute-start(bf16[64,4096]{1,0:T(8,128)(2,1)S(1)} %bitcast.24), channel_id=1, source_target_pairs={{0,64},{1,25},{2,66},{3,27},{4,68},{5,29},{6,70},{7,31},{8,72},{9,... | collective-permute-start | bytes 1572872 | tf_op jit(solution)/shard_map/ppermute | solution.py:57
  67.4 0.0 collective-permute-done.refs_1_
  67.4 4.0 %collective-permute-start.4 = (bf16[64,4096]{1,0:T(8,128)(2,1)S(1)}, bf16[64,4096]{1,0:T(8,128)(2,1)S(1)}, u32[]{:S(2)}, u32[]{:S(2)}) collective-permute-start(bf16[64,4096]{1,0:T(8,128)(2,1)S(1)} %collective-permute-done.refs_1_), channel_id=1, source_target_pairs={{0,64},{1,25},{2,66},{3,27},{4,68},{5,29},{6,70},{7,31},{8,72},{9,... | collective-permute-start | bytes 1572872 | tf_op jit(solution)/shard_map/ppermute | solution.py:57
  71.4 0.0 collective-permute-done.3.refs_1_
  71.4 4.6 %collective-permute-start.5 = (bf16[64,4096]{1,0:T(8,128)(2,1)S(1)}, bf16[64,4096]{1,0:T(8,128)(2,1)S(1)}, u32[]{:S(2)}, u32[]{:S(2)}) collective-permute-start(bf16[64,4096]{1,0:T(8,128)(2,1)S(1)} %collective-permute-done.3.refs_1_), channel_id=1, source_target_pairs={{0,8},{1,449},{2,10},{3,451},{4,12},{5,453},{6,14},{7,455},{8,0},{... | collective-permute-start | bytes 1572872 | tf_op jit(solution)/shard_map/ppermute | solution.py:57
  76.0 2.5 %shard_map.48.refs_3_.refs_4_ = bf16[512,4096]{1,0:T(8,128)(2,1)S(1)} custom-call(bf16[512,32,128]{2,1,0:T(8,128)(2,1)} %bitcast.21), custom_call_target="tpu_custom_call" | custom-call | bytes 8388608 | tf_op jit(solution)/shard_map/pallas_call | solution.py:140
  78.5 0.0 collective-permute-done.1.refs_2_
  78.5 1.3 %shard_map.49 = (f32[128,512]{1,0:T(8,128)S(1)}, f32[128,512]{1,0:T(8,128)S(1)}) custom-call(bf16[128,4096]{1,0:T(8,128)(2,1)S(1)} %bitcast.15, bf16[64,4096]{1,0:T(8,128)(2,1)S(1)} %collective-permute-done.refs_1_, bf16[64,4096]{1,0:T(8,128)(2,1)S(1)} %collective-permute-done.1.refs_2_, bf16[512,4096]{1,0:T(8,128)(2,1)S(1)} %shard_map.48.refs_3_.refs_4_), custom_call_target="tpu_custom_call" | custom-call | flops 1073741824 | bytes 6291456 | tf_op jit(solution)/shard_map/pallas_call | solution.py:171
  79.9 3.4 %all-gather.1 = f32[256,512]{1,0:T(8,128)S(1)} all-gather(f32[128,512]{1,0:T(8,128)S(1)} %get-tuple-element.19), channel_id=3, replica_groups=mesh['zh'=2,'zl'=4,'yl'=2,'x'=4,'yh'=4,'c'=2] {'c'}, dimensions={0}, use_global_device_ids=true | all-gather | bytes 786432 | tf_op jit(solution)/shard_map/all_gather | solution.py:261
  83.3 0.0 collective-permute-done.2.refs_0_
  83.3 0.0 collective-permute-done.4.refs_2_
  83.3 0.0 collective-permute-done.5.refs_3_
  83.3 1.3 %shard_map.50 = (f32[128,512]{1,0:T(8,128)S(1)}, f32[128,512]{1,0:T(8,128)S(1)}) custom-call(bf16[64,4096]{1,0:T(8,128)(2,1)S(1)} %collective-permute-done.2.refs_0_, bf16[64,4096]{1,0:T(8,128)(2,1)S(1)} %collective-permute-done.3.refs_1_, bf16[64,4096]{1,0:T(8,128)(2,1)S(1)} %collective-permute-done.4.refs_2_, ...), custom_call_target="tpu_custom_call" | custom-call | flops 1073741824 | bytes 6291456 | tf_op jit(solution)/shard_map/pallas_call | solution.py:171
  84.7 3.9 %all-gather.2 = f32[256,512]{1,0:T(8,128)S(1)} all-gather(f32[128,512]{1,0:T(8,128)S(1)} %get-tuple-element.20), channel_id=4, replica_groups=mesh['zh'=2,'zl'=4,'yl'=2,'x'=4,'yh'=4,'c'=2] {'c'}, dimensions={0}, use_global_device_ids=true | all-gather | bytes 786432 | tf_op jit(solution)/shard_map/all_gather | solution.py:263
  88.6 0.1 shard_map.51
  88.7 12.3 %all_to_all.17.parts_ref = bf16[4,4,16,512]{3,2,1,0:T(8,128)(2,1)S(1)} all-to-all(bf16[4,4,16,512]{3,2,1,0:T(8,128)(2,1)S(1)} %bitcast.20), channel_id=1, replica_groups=mesh['zh'=2,'zl'=4,'yl'=2,'x'=4,'yh'=4,'c'=2] {'yh'}, dimensions={0} | all-to-all | bytes 524288 | tf_op jit(solution)/shard_map/all_to_all | solution.py:265
  101.0 0.7 shard_map.52
Async XLA Ops:
  49.8 17.6 %collective-permute-start = (bf16[64,4096]{1,0:T(8,128)(2,1)S(1)}, bf16[64,4096]{1,0:T(8,128)(2,1)S(1)}, u32[]{:S(2)}, u32[]{:S(2)}) collective-permute-start(bf16[64,4096]{1,0:T(8,128)(2,1)S(1)} %bitcast.23), channel_id=1, source_target_pairs={{0,8},{1,449},{2,10},{3,451},{4,12},{5,453},{6,14},{7,455},{8,0},{... | collective-permute-start | bytes 1572872 | tf_op jit(solution)/shard_map/ppermute | solution.py:57
  58.9 12.5 %collective-permute-start.3 = (bf16[64,4096]{1,0:T(8,128)(2,1)S(1)}, bf16[64,4096]{1,0:T(8,128)(2,1)S(1)}, u32[]{:S(2)}, u32[]{:S(2)}) collective-permute-start(bf16[64,4096]{1,0:T(8,128)(2,1)S(1)} %bitcast.25), channel_id=1, source_target_pairs={{0,64},{1,25},{2,66},{3,27},{4,68},{5,29},{6,70},{7,31},{8,72},{9,... | collective-permute-start | bytes 1572872 | tf_op jit(solution)/shard_map/ppermute | solution.py:57
  62.9 15.6 %collective-permute-start.1 = (bf16[64,4096]{1,0:T(8,128)(2,1)S(1)}, bf16[64,4096]{1,0:T(8,128)(2,1)S(1)}, u32[]{:S(2)}, u32[]{:S(2)}) collective-permute-start(bf16[64,4096]{1,0:T(8,128)(2,1)S(1)} %bitcast.26), channel_id=1, source_target_pairs={{0,8},{1,449},{2,10},{3,451},{4,12},{5,453},{6,14},{7,455},{8,0},{... | collective-permute-start | bytes 1572872 | tf_op jit(solution)/shard_map/ppermute | solution.py:57
  64.9 18.4 %collective-permute-start.2 = (bf16[64,4096]{1,0:T(8,128)(2,1)S(1)}, bf16[64,4096]{1,0:T(8,128)(2,1)S(1)}, u32[]{:S(2)}, u32[]{:S(2)}) collective-permute-start(bf16[64,4096]{1,0:T(8,128)(2,1)S(1)} %bitcast.24), channel_id=1, source_target_pairs={{0,64},{1,25},{2,66},{3,27},{4,68},{5,29},{6,70},{7,31},{8,72},{9,... | collective-permute-start | bytes 1572872 | tf_op jit(solution)/shard_map/ppermute | solution.py:57
  67.4 15.9 %collective-permute-start.4 = (bf16[64,4096]{1,0:T(8,128)(2,1)S(1)}, bf16[64,4096]{1,0:T(8,128)(2,1)S(1)}, u32[]{:S(2)}, u32[]{:S(2)}) collective-permute-start(bf16[64,4096]{1,0:T(8,128)(2,1)S(1)} %collective-permute-done.refs_1_), channel_id=1, source_target_pairs={{0,64},{1,25},{2,66},{3,27},{4,68},{5,29},{6,70},{7,31},{8,72},{9,... | collective-permute-start | bytes 1572872 | tf_op jit(solution)/shard_map/ppermute | solution.py:57
  71.4 11.9 %collective-permute-start.5 = (bf16[64,4096]{1,0:T(8,128)(2,1)S(1)}, bf16[64,4096]{1,0:T(8,128)(2,1)S(1)}, u32[]{:S(2)}, u32[]{:S(2)}) collective-permute-start(bf16[64,4096]{1,0:T(8,128)(2,1)S(1)} %collective-permute-done.3.refs_1_), channel_id=1, source_target_pairs={{0,8},{1,449},{2,10},{3,451},{4,12},{5,453},{6,14},{7,455},{8,0},{... | collective-permute-start | bytes 1572872 | tf_op jit(solution)/shard_map/ppermute | solution.py:57
